TPU v7x, 512 devices: a whole 4x8x8 slice. The times are simulated.
512 devices in a mesh: ctx: 64 (over x, y, core), split: 8 (over z).
Axes of the slice: x: 4, y: 8, z: 8, core: 2. Of those that a mesh axis runs over, the one named last changes fastest.
Arguments:
- cache_keys: bfloat16 [64, 1024, 64, 128], P(None, ('ctx', 'split')), may hold values from -5 to 5
- cache_values: bfloat16 [64, 1024, 64, 128], P(None, ('ctx', 'split')), may hold values from -6 to 6
- counts: int32 [16, 1024], replicated, may hold values from 1 to 64, as said below
- listed: int32 [64, 256], replicated, may hold values from 0 to 1023, as said below
- queries: bfloat16 [64, 128, 16, 128], P('ctx'), may hold values from -100 to 100
Outputs:
- attended: float32 [64, 128, 16, 128], P('ctx')
Inputs may be any that keep to these rules, and one draw needn't show every extreme that they name: listed[i] holds 256 distinct pages; of the 2 pages of one device (pages d * 2 to d * 2 + 1 of device d in ctx-major order) at most one is listed for an item; for every item all devices of one split index hold a listed page. Slots 0 to counts - 1 of a page are valid; the first listed page of every item is full.
All inputs are finite; a program needn't handle non-finite values.
Results may differ from a plain program's by a relative error of at most 0.005.
Values may be sent and summed in bfloat16 or wider, within the bound.
No kernel may reach another device: no remote copies, remote signals or barrier semaphores. Data moves between devices by JAX's collectives and lax.ppermute only.
A program may use at most 64 MiB of HBM per device.

v0:
```python
import jax
import jax.numpy as jnp
from jax import lax
from jax.sharding import PartitionSpec as P

NEG = -1e30


def local(cache_keys, cache_values, counts, listed, queries):
    ctx_n = lax.axis_size("ctx")
    split_n = lax.axis_size("split")
    items, pages_here, page_len, head = cache_keys.shape
    kv_heads = items // counts.shape[0]
    scale = head ** (-0.5)
    tok = jnp.arange(page_len, dtype=jnp.int32)
    split_idx = lax.axis_index("split")
    here = (lax.axis_index("ctx") * split_n + split_idx) * pages_here + jnp.arange(
        pages_here, dtype=jnp.int32
    )
    local_counts = lax.dynamic_slice_in_dim(counts, here[0], pages_here, 1)
    local_counts = jnp.repeat(local_counts, kv_heads, axis=0)
    valid = (tok[None, None, :] < local_counts[:, :, None]).astype(jnp.bfloat16)
    count_f = local_counts.astype(jnp.float32)[:, :, None]
    key_sums = jnp.einsum("ipt,iptd->ipd", valid, cache_keys, preferred_element_type=jnp.float32)
    value_sums = jnp.einsum(
        "ipt,iptd->ipd", valid, cache_values, preferred_element_type=jnp.float32
    )
    mean_keys = (key_sums / count_f).astype(jnp.bfloat16)
    mean_values = (value_sums / count_f).astype(jnp.bfloat16)
    got_keys, got_values = (
        lax.all_to_all(mean_keys, "ctx", split_axis=0, concat_axis=1, tiled=True),
        lax.all_to_all(mean_values, "ctx", split_axis=0, concat_axis=1, tiled=True),
    )
    cent_keys = got_keys[0]
    cent_values = got_values[0]
    item = lax.axis_index("ctx")
    sel_row = lax.dynamic_slice_in_dim(listed, item, 1, 0)[0]
    count_row = lax.dynamic_slice_in_dim(counts, item // kv_heads, 1, 0)[0]
    sources = jnp.arange(ctx_n, dtype=jnp.int32)
    candidate = (sources * split_n + split_idx)[:, None] * pages_here + jnp.arange(
        pages_here, dtype=jnp.int32
    )[None, :]
    marks = jnp.any(sel_row[None, None, :] == candidate[:, :, None], axis=2)
    cand_counts = jnp.take(count_row, candidate)
    recv_keys, recv_values = (
        lax.all_to_all(cache_keys, "ctx", split_axis=0, concat_axis=1, tiled=True),
        lax.all_to_all(cache_values, "ctx", split_axis=0, concat_axis=1, tiled=True),
    )
    pick = marks.astype(jnp.bfloat16)
    shaped = (ctx_n, pages_here, page_len, head)
    page_keys = jnp.einsum(
        "cl,clte->cte", pick, recv_keys[0].reshape(shaped), preferred_element_type=jnp.float32
    ).astype(jnp.bfloat16)
    page_values = jnp.einsum(
        "cl,clte->cte", pick, recv_values[0].reshape(shaped), preferred_element_type=jnp.float32
    ).astype(jnp.bfloat16)
    slot_count = jnp.sum(jnp.where(marks, cand_counts, 0), axis=1)
    live = tok[None, :] < slot_count[:, None]
    rows = queries.reshape(-1, head)
    contract = (((1,), (1,)), ((), ()))
    open_pages = jnp.logical_not(marks.reshape(-1))
    log_counts = jnp.log(cand_counts.reshape(-1).astype(jnp.float32))
    cscore = (
        lax.dot_general(rows, cent_keys, contract, preferred_element_type=jnp.float32) * scale
        + log_counts[None, :]
    )
    cscore = jnp.where(open_pages[None, :], cscore, NEG)
    start_max = jnp.max(cscore, axis=1)
    cweight = jnp.where(open_pages[None, :], jnp.exp(cscore - start_max[:, None]), 0.0)
    start_total = jnp.sum(cweight, axis=1)
    start_out = jnp.dot(
        cweight.astype(jnp.bfloat16), cent_values, preferred_element_type=jnp.float32
    )
    block = min(ctx_n, max(1, 512 // page_len))
    blocks = ctx_n // block
    block_keys = page_keys.reshape(blocks, block * page_len, head)
    block_values = page_values.reshape(blocks, block * page_len, head)
    block_live = live.reshape(blocks, block * page_len)

    def attend(carry, piece):
        top, total, weighted = carry
        keys_b, values_b, live_b = piece
        score = lax.dot_general(rows, keys_b, contract, preferred_element_type=jnp.float32) * scale
        score = jnp.where(live_b[None, :], score, NEG)
        new_top = jnp.maximum(top, jnp.max(score, axis=1))
        shrink = jnp.exp(top - new_top)
        weight = jnp.where(live_b[None, :], jnp.exp(score - new_top[:, None]), 0.0)
        total = total * shrink + jnp.sum(weight, axis=1)
        weighted = weighted * shrink[:, None] + jnp.dot(
            weight.astype(jnp.bfloat16), values_b, preferred_element_type=jnp.float32
        )
        return ((new_top, total, weighted), None)

    state, unused = lax.scan(
        attend, (start_max, start_total, start_out), (block_keys, block_values, block_live)
    )
    top, total, weighted = state
    whole_top = lax.pmax(top, "split")
    factor = jnp.exp(top - whole_top)
    whole_total, whole_out = lax.psum((total * factor, weighted * factor[:, None]), "split")
    return (whole_out / whole_total[:, None]).reshape(queries.shape)


def solution(mesh):
    return jax.shard_map(
        local,
        mesh=mesh,
        in_specs=(
            P(None, ("ctx", "split"), None, None),
            P(None, ("ctx", "split"), None, None),
            P(),
            P(),
            P("ctx", None, None, None),
        ),
        out_specs=P("ctx", None, None, None),
        check_vma=False,
    )
```

profile of v0, /device:TPU:1, one launch (start us, length us, event | category | flops | bytes accessed | tf_op | source)
XLA Modules:
  0.0 309.8 jit_solution(8601471895384795277)
XLA Ops:
  7.9 2.2 fusion.31
  10.2 2.2 fusion.33
  12.7 20.7 %all_to_all.16 = bf16[64,2,128]{2,1,0:T(2,128)(2,1)S(1)} all-to-all(bf16[64,2,128]{2,1,0:T(2,128)(2,1)S(1)} %get-tuple-element.75), channel_id=1, replica_groups=mesh['ctx'=64,'split'=8] {'ctx'}, dimensions={0} | all-to-all | bytes 65536 | tf_op jit(solution)/shard_map/all_to_all | solution.py:31
  33.4 13.3 %all_to_all.17 = bf16[64,2,128]{2,1,0:T(2,128)(2,1)S(1)} all-to-all(bf16[64,2,128]{2,1,0:T(2,128)(2,1)S(1)} %get-tuple-element.74), channel_id=1, replica_groups=mesh['ctx'=64,'split'=8] {'ctx'}, dimensions={0} | all-to-all | bytes 65536 | tf_op jit(solution)/shard_map/all_to_all | solution.py:32
  46.7 55.9 %all_to_all.18 = bf16[64,2,64,128]{3,2,1,0:T(8,128)(2,1)} all-to-all(bf16[64,2,64,128]{3,2,1,0:T(8,128)(2,1)S(1)} %copy-done.2), channel_id=1, replica_groups=mesh['ctx'=64,'split'=8] {'ctx'}, dimensions={0} | all-to-all | bytes 4194304 | tf_op jit(solution)/shard_map/all_to_all | solution.py:46
  102.6 6.0 %all-to-all-start.3 = ((bf16[64,2,64,128]{3,2,1,0:T(8,128)(2,1)}), bf16[64,2,64,128]{3,2,1,0:T(8,128)(2,1)}, u32[]{:S(2)}, u32[]{:S(2)}) async-start(bf16[64,2,64,128]{3,2,1,0:T(8,128)(2,1)} %param.8), calls=%async_computation.3 | async-start | bytes 4194304 | tf_op jit(solution)/shard_map/all_to_all | solution.py:47
  113.4 3.9 %fusion.22 = f32[64,1,64,128]{3,1,2,0:T(1,128)S(1)} fusion(pred[64,2,1,1]{1,2,3,0:T(4,128)(4,1)S(1)} %copy.21, bf16[64,2,64,128]{3,2,1,0:T(8,128)(2,1)} %all_to_all.18), kind=kOutput, calls=%fused_computation.29 | convolution fusion | flops 2097152 | bytes 4194432 | tf_op jit(solution)/shard_map/cl,clte->cte/dot_general | solution.py:51
  117.5 42.3 %all-to-all-done.3 = bf16[64,2,64,128]{3,2,1,0:T(8,128)(2,1)} async-done(((bf16[64,2,64,128]{3,2,1,0:T(8,128)(2,1)}), bf16[64,2,64,128]{3,2,1,0:T(8,128)(2,1)}, u32[]{:S(2)}, u32[]{:S(2)}) %all-to-all-start.3) | async-done | bytes 2097184 | tf_op jit(solution)/shard_map/all_to_all | solution.py:47
  159.8 3.9 %fusion.20 = f32[64,1,64,128]{3,1,2,0:T(1,128)S(1)} fusion(pred[64,2,1,1]{1,2,3,0:T(4,128)(4,1)S(1)} %copy.21, bf16[64,2,64,128]{3,2,1,0:T(8,128)(2,1)} %all-to-all-done.3), kind=kOutput, calls=%fused_computation.27 | convolution fusion | flops 2097152 | bytes 4194432 | tf_op jit(solution)/shard_map/cl,clte->cte/dot_general | solution.py:54
  164.9 40.1 %while.14 = (s32[]{:T(128)}, f32[2048]{0:T(1024)S(1)}, f32[2048]{0:T(1024)S(1)}, f32[2048,128]{1,0:T(8,128)S(1)}, pred[8,512]{1,0:T(8,128)(4,1)S(1)}, /*index=5*...) while((s32[]{:T(128)}, f32[2048]{0:T(1024)S(1)}, ...), condition=%wide.region_7.8_spmd, body=%wide.region_4.7_spmd.sunk | while | flops 551030784 | bytes 15600741 | solution.py:94
  165.7 1.3 fusion.57
  167.0 2.9 convolution_add_fusion.2
  172.0 2.9 convolution_add_fusion.2
  177.0 2.9 convolution_add_fusion.2
  182.0 2.9 convolution_add_fusion.2
  187.1 2.9 convolution_add_fusion.2
  192.1 2.9 convolution_add_fusion.2
  197.1 2.9 convolution_add_fusion.2
  202.1 2.9 convolution_add_fusion.2
  205.0 19.7 %pmax.7 = f32[2048]{0:T(1024)S(1)} all-reduce(f32[2048]{0:T(1024)S(1)} %get-tuple-element.50), channel_id=1, replica_groups=mesh['ctx'=64,'split'=8] {'split'}, use_global_device_ids=true, to_apply=%region_8.9 | all-reduce | flops 2048 | bytes 16384 | tf_op jit(solution)/shard_map/pmax | solution.py:98
  224.7 1.3 broadcast_multiply_fusion
  226.0 10.9 %psum.15 = f32[2048]{0:T(1024)S(1)} all-reduce(f32[2048]{0:T(1024)S(1)} %get-tuple-element.70), channel_id=1, replica_groups=mesh['ctx'=64,'split'=8] {'split'}, use_global_device_ids=true, to_apply=%region_10.11 | all-reduce | flops 2048 | bytes 16384 | tf_op jit(solution)/shard_map/psum | solution.py:100
  237.0 63.4 %all-reduce.2.cloned.1.call-done = f32[2048,128]{1,0:T(8,128)} async-done(((f32[2048,128]{1,0:T(8,128)}), f32[2048,128]{1,0:T(8,128)}) %all-reduce.2.cloned.1.call-update) | async-done | bytes 1048592 | tf_op jit(solution)/shard_map/psum | solution.py:100
  300.4 2.5 broadcast_divide_fusion
  (98 shorter events, 22.9 us)
Async XLA Ops:
  6.5 0.8 copy-start
  6.5 40.1 %copy-start.2 = (bf16[64,2,64,128]{3,2,1,0:T(8,128)(2,1)S(1)}, bf16[64,2,64,128]{3,2,1,0:T(8,128)(2,1)}, u32[]{:S(2)}) copy-start(bf16[64,2,64,128]{3,2,1,0:T(8,128)(2,1)} %param.7) | copy-start | bytes 6291460
  102.6 57.2 %all-to-all-start.3 = ((bf16[64,2,64,128]{3,2,1,0:T(8,128)(2,1)}), bf16[64,2,64,128]{3,2,1,0:T(8,128)(2,1)}, u32[]{:S(2)}, u32[]{:S(2)}) async-start(bf16[64,2,64,128]{3,2,1,0:T(8,128)(2,1)} %param.8), calls=%async_computation.3 | async-start | bytes 4194304 | tf_op jit(solution)/shard_map/all_to_all | solution.py:47
  108.6 191.7 %all-reduce.2.cloned.1.call-start = ((), (), s32[]{:S(2)}) async-start(), calls=%async_computation.4 | async-start | bytes 2097152 | tf_op jit(solution)/shard_map/psum | solution.py:100
  110.7 1.7 copy-start.1
Sparse Core Ops, SparseCore 0:
  226.1 74.2 all-reduce.1
where the time goes:
time: 313 us; the launch traced here: 310 us
  blocking collectives  121 us (39%)
  waiting for transfers between devices  106 us (34%)
  matrix products  42.1 us (13%)
  other arithmetic  16.4 us (5%)
  between operations  13.7 us (4%)
  starting transfers between devices  6.23 us (2%)
  local copies, waits for them, and re-layouts  4.58 us (1%)
    psum x1, waiting for transfers between devices, local(): lax.psum((total * factor, weighted * factor[:, None]), 'split')  63.4 us
    all_to_all x1, blocking collectives, local(): lax.all_to_all(cache_keys, 'ctx', split_axis=0, concat_axis=1, tiled=True)  55.9 us
    all_to_all x1, waiting for transfers between devices, local(): lax.all_to_all(cache_values, 'ctx', split_axis=0, concat_axis=1, tiled=True)  42.3 us
    dot_general x8, matrix products, attend(): jnp.dot(weight.astype(jnp.bfloat16), values_b, preferred_element_type=jnp...  23 us
    all_to_all x1, blocking collectives, local(): lax.all_to_all(mean_keys, 'ctx', split_axis=0, concat_axis=1, tiled=True)  20.7 us
    pmax x1, blocking collectives, local(): whole_top = lax.pmax(top, 'split')  19.7 us
    all_to_all x1, blocking collectives, local(): lax.all_to_all(mean_values, 'ctx', split_axis=0, concat_axis=1, tiled=True)  13.3 us
    psum x1, blocking collectives, local(): lax.psum((total * factor, weighted * factor[:, None]), 'split')  10.9 us
  transfers between devices with their start and end apart: 2, of which 2 were waited for; matrix products, arithmetic and copies ran while one was open for 3% of the time, Pallas kernels for 0%

commit v1 on v0

v1 whole, which is shorter than its diff:
```python
import functools

import jax
import jax.numpy as jnp
from jax import lax
from jax.experimental import pallas as pl
from jax.experimental.pallas import tpu as pltpu
from jax.sharding import PartitionSpec as P

NEG = -1e30
LOG2E = 1.4426950408889634

PAGE = 64
HEAD = 128
TAIL = 8
ROWS = 2 * PAGE + TAIL
MiB = 1024 * 1024


def pack_kernel(page_ref, count_ref, listed_ref, keys_ref, values_ref, out_ref, cache, message, got, sent):
    items = out_ref.shape[0]
    kv_heads = 4
    block = 8
    groups = items // block

    def fetch(g):
        at = pl.ds(g * block, block)
        return [
            pltpu.make_async_copy(ref.at[at], cache.at[at, a], got.at[a, g])
            for a, ref in enumerate((keys_ref, values_ref))
        ]

    def send(g):
        at = pl.ds(g * block, block)
        return pltpu.make_async_copy(message.at[at], out_ref.at[at], sent.at[g])

    for g in range(groups):
        for copy in fetch(g):
            copy.start()
    second = jnp.max(
        jnp.where(listed_ref[...] == page_ref[0] + 1, 1.0, 0.0), axis=1, keepdims=True
    )
    row = lax.broadcasted_iota(jnp.int32, (16, 4 * PAGE), 0)
    slot = lax.broadcasted_iota(jnp.int32, (16, 4 * PAGE), 1)
    quarter = slot // PAGE
    slot = slot % PAGE
    out_row = lax.broadcasted_iota(jnp.int32, (16, HEAD), 0)
    for g in range(groups):
        for copy in fetch(g):
            copy.wait()
        for item in range(g * block, (g + 1) * block):
            if item % kv_heads == 0:
                request = item // kv_heads
                count = [count_ref[2 * request], count_ref[2 * request + 1]]
                limit = jnp.where(row % 2 == 0, count[0], count[1])
                live = jnp.logical_and(quarter == row, slot < limit)
                live = jnp.where(live, 1.0, 0.0).astype(jnp.bfloat16)
                divisor = jnp.where(out_row % 2 == 0, count[0], count[1]).astype(jnp.float32)
                inverse = 1.0 / divisor
            choice = jnp.broadcast_to(second[item : item + 1, :], (PAGE, HEAD)) > 0.5
            for a in range(2):
                message[item, a * PAGE : (a + 1) * PAGE, :] = jnp.where(
                    choice, cache[item, a, 1], cache[item, a, 0]
                )
            both = cache[item].reshape(4 * PAGE, HEAD)
            total = jnp.dot(live, both, preferred_element_type=jnp.float32)
            message[item, 2 * PAGE : ROWS, :] = (total * inverse)[:TAIL].astype(jnp.bfloat16)
        send(g).start()
    for g in range(groups):
        send(g).wait()


def pack(page, local_counts, listed, cache_keys, cache_values):
    items = cache_keys.shape[0]
    groups = items // 8
    whole = pl.BlockSpec(memory_space=pl.ANY)
    scalars = pl.BlockSpec(memory_space=pltpu.SMEM)
    return pl.pallas_call(
        pack_kernel,
        in_specs=[scalars, scalars, pl.BlockSpec(memory_space=pltpu.VMEM), whole, whole],
        out_specs=whole,
        out_shape=jax.ShapeDtypeStruct((items, ROWS, HEAD), jnp.bfloat16),
        scratch_shapes=[
            pltpu.VMEM((items, 2, 2, PAGE, HEAD), jnp.bfloat16),
            pltpu.VMEM((items, ROWS, HEAD), jnp.bfloat16),
            pltpu.SemaphoreType.DMA((2, groups)),
            pltpu.SemaphoreType.DMA((groups,)),
        ],
        compiler_params=pltpu.CompilerParams(vmem_limit_bytes=58 * MiB),
        name="pack",
    )(page, local_counts, listed, cache_keys, cache_values)


def split3(x):
    high = x.astype(jnp.bfloat16).astype(jnp.float32)
    rest = x - high
    middle = rest.astype(jnp.bfloat16).astype(jnp.float32)
    return high, middle, rest - middle


def attend_kernel(
    live_ref, cbias_ref, got_ref, q_ref, out_ref, ka, vv, vt, qt, sc0, sc1, acc, *, chunk, c2
):
    sources = got_ref.shape[0]
    cents = 2 * sources
    block = qt.shape[2]
    width = out_ref.shape[2]
    blocks = q_ref.shape[0] // block
    sc = (sc0, sc1)
    lane = lax.broadcasted_iota(jnp.int32, (PAGE, HEAD), 1)
    tok = lax.broadcasted_iota(jnp.int32, (PAGE, HEAD), 0)
    vt[HEAD:, :] = jnp.ones((vt.shape[0] - HEAD, vt.shape[1]), jnp.bfloat16)
    for i in range(2):
        qt[i, HEAD:, :] = jnp.ones((HEAD, block), jnp.bfloat16)

    tails = got_ref[:, 2 * PAGE : ROWS, :].astype(jnp.float32).reshape(sources * TAIL, HEAD)
    tails = tails.astype(jnp.bfloat16)
    r = lax.broadcasted_iota(jnp.int32, (cents, sources * TAIL), 0)
    c = lax.broadcasted_iota(jnp.int32, (cents, sources * TAIL), 1)
    first = (r // 2) * TAIL + r % 2
    for off, ref in ((0, ka), (2, vv)):
        chosen = (c == first + off).astype(jnp.float32).astype(jnp.bfloat16)
        ref[0:cents, :HEAD] = jnp.dot(
            chosen, tails, preferred_element_type=jnp.float32
        ).astype(jnp.bfloat16)
    high, middle, low = split3(jnp.transpose(jnp.broadcast_to(cbias_ref[...], (cents, cents))))
    clane = lax.broadcasted_iota(jnp.int32, (cents, HEAD), 1)
    bias = jnp.where(clane == 0, high, jnp.where(clane == 1, middle, low))
    ka[0:cents, HEAD:] = jnp.where(clane < 3, bias, 0.0).astype(jnp.bfloat16)

    def place(s, at):
        rows = pl.ds(pl.multiple_of(at, 16), PAGE)
        live = live_ref[s]
        ka[rows, :HEAD] = got_ref[s, 0:PAGE, :]
        vv[rows, :] = got_ref[s, PAGE : 2 * PAGE, :]
        dead = jnp.logical_and(lane == 0, tok >= live)
        ka[rows, HEAD:] = jnp.where(dead, NEG, 0.0).astype(jnp.bfloat16)
        return at + ((live + 15) // 16) * 16

    end = lax.fori_loop(0, sources, place, cents)
    dead = jnp.where(lane == 0, NEG, 0.0).astype(jnp.bfloat16)
    for k in range(0, chunk, PAGE):
        rows = pl.ds(pl.multiple_of(end + k, 16), PAGE)
        ka[rows, :HEAD] = jnp.zeros((PAGE, HEAD), jnp.bfloat16)
        ka[rows, HEAD:] = dead
        vv[rows, :] = jnp.zeros((PAGE, HEAD), jnp.bfloat16)
    chunks = (end + chunk - 1) // chunk

    def turn(j, carry):
        for k in range(0, chunk, HEAD):
            at = pl.ds(pl.multiple_of(j * chunk + k, HEAD), HEAD)
            vt[:HEAD, at] = jnp.transpose(vv[at, :].astype(jnp.float32)).astype(jnp.bfloat16)
        return carry

    lax.fori_loop(0, chunks, turn, 0)

    top = None
    for b in range(blocks + 1):
        if b < blocks:
            rows = q_ref[b * block : (b + 1) * block, :].astype(jnp.float32)
            qt[b % 2, :HEAD, :] = jnp.transpose(rows).astype(jnp.bfloat16)
        if b > 0:
            acc[...] = jnp.zeros_like(acc)

        def body(j, best, b=b, top=top):
            at = pl.ds(pl.multiple_of(j * chunk, chunk), chunk)
            if b > 0:
                weight = jnp.exp2((sc[(b - 1) % 2][at, :] - top) * c2).astype(jnp.bfloat16)
                acc[...] += jnp.dot(vt[:, at], weight, preferred_element_type=jnp.float32)
            if b < blocks:
                score = jnp.dot(ka[at, :], qt[b % 2], preferred_element_type=jnp.float32)
                sc[b % 2][at, :] = score
                best = jnp.maximum(best, jnp.max(score.reshape(chunk // 8, 8, block), axis=0))
            return best

        best = lax.fori_loop(0, chunks, body, jnp.full((8, block), 4 * NEG, jnp.float32))
        if b > 0:
            total = acc[HEAD : HEAD + 1, :]
            out = (acc[:HEAD, :] / total).astype(jnp.bfloat16)
            row = lax.broadcasted_iota(jnp.int32, (TAIL, block), 0)
            tile = jnp.zeros((TAIL, block), jnp.float32)
            for i, piece in enumerate(split3(top) + split3(total)):
                tile = jnp.where(row == i, piece, tile)
            tile = tile.astype(jnp.bfloat16)
            for k in range(block // width):
                to = (b - 1) * (block // width) + k
                out_ref[to, :HEAD, :] = out[:, k * width : (k + 1) * width]
                out_ref[to, HEAD:, :] = tile[:, k * width : (k + 1) * width]
        top = jnp.max(best, axis=0, keepdims=True)


def attend(live, cbias, got, rows, parts, c2):
    sources = got.shape[0]
    chunk = 512
    block = 512
    keys = sources * (PAGE + 2)
    padded = pl.cdiv(keys, chunk) * chunk
    width = rows.shape[0] // parts
    vmem = pl.BlockSpec(memory_space=pltpu.VMEM)
    return pl.pallas_call(
        functools.partial(attend_kernel, chunk=chunk, c2=c2),
        in_specs=[pl.BlockSpec(memory_space=pltpu.SMEM), vmem, vmem, vmem],
        out_specs=vmem,
        scratch_shapes=[
            pltpu.VMEM((padded + chunk, 2 * HEAD), jnp.bfloat16),
            pltpu.VMEM((padded + chunk, HEAD), jnp.bfloat16),
            pltpu.VMEM((HEAD + 16, padded), jnp.bfloat16),
            pltpu.VMEM((2, 2 * HEAD, block), jnp.bfloat16),
            pltpu.VMEM((padded, block), jnp.float32),
            pltpu.VMEM((padded, block), jnp.float32),
            pltpu.VMEM((HEAD + 16, block), jnp.float32),
        ],
        out_shape=jax.ShapeDtypeStruct((parts, HEAD + TAIL, width), jnp.bfloat16),
        compiler_params=pltpu.CompilerParams(vmem_limit_bytes=36 * MiB),
        cost_estimate=pl.CostEstimate(
            flops=4 * rows.shape[0] * keys * HEAD,
            bytes_accessed=4 * MiB,
            transcendentals=rows.shape[0] * keys,
        ),
        name="attend",
    )(live, cbias, got, rows)


def merge_kernel(got_ref, out_ref, *, c2):
    parts = got_ref.shape[0]
    tops, totals = [], []
    for z in range(parts):
        tile = got_ref[z, HEAD:, :].astype(jnp.float32)
        tops.append(tile[0:1] + tile[1:2] + tile[2:3])
        totals.append(tile[3:4] + tile[4:5] + tile[5:6])
    top = functools.reduce(jnp.maximum, tops)
    factors = [t * jnp.exp2((m - top) * c2) for m, t in zip(tops, totals)]
    whole = functools.reduce(jnp.add, factors)
    out = jnp.zeros(got_ref.shape[1:], jnp.float32)[:HEAD]
    for z in range(parts):
        out += got_ref[z, :HEAD, :].astype(jnp.float32) * (factors[z] / whole)
    out = jnp.transpose(out).astype(jnp.bfloat16)
    for z in range(parts):
        out_ref[z] = out


def merge(got, c2):
    parts, unused, block = got.shape
    return pl.pallas_call(
        functools.partial(merge_kernel, c2=c2),
        out_shape=jax.ShapeDtypeStruct((parts, block, HEAD), jnp.bfloat16),
        compiler_params=pltpu.CompilerParams(vmem_limit_bytes=16 * MiB),
        name="merge",
    )(got)


def local(cache_keys, cache_values, counts, listed, queries):
    ctx_n = lax.axis_size("ctx")
    split_n = lax.axis_size("split")
    items, pages_here, page_len, head = cache_keys.shape
    requests = counts.shape[0]
    kv_heads = items // requests
    root = head**0.5
    c2 = head**-0.5 * LOG2E
    item = lax.axis_index("ctx")
    split_idx = lax.axis_index("split")
    first = (item * split_n + split_idx) * pages_here
    local_counts = lax.dynamic_slice_in_dim(counts, first, pages_here, 1).reshape(-1)
    message = pack(first.reshape(1), local_counts, listed, cache_keys, cache_values)
    got = lax.all_to_all(message, "ctx", split_axis=0, concat_axis=0, tiled=True)

    sel_row = lax.dynamic_index_in_dim(listed, item, 0, keepdims=False)
    count_row = lax.dynamic_index_in_dim(counts, item // kv_heads, 0, keepdims=False)
    mine = count_row.reshape(ctx_n, split_n, pages_here)
    mine = lax.dynamic_index_in_dim(mine, split_idx, 1, keepdims=False)
    source = jnp.arange(ctx_n, dtype=jnp.int32)[:, None]
    candidate = (source * split_n + split_idx) * pages_here + jnp.arange(
        pages_here, dtype=jnp.int32
    )
    marks = jnp.any(sel_row[None, None, :] == candidate[:, :, None], axis=2)
    live = jnp.sum(jnp.where(marks, mine, 0), axis=1)
    cbias = jnp.where(marks, NEG, jnp.log(mine.astype(jnp.float32)) * root)
    rows = queries.reshape(-1, head)
    partial = attend(live, cbias.reshape(1, -1), got, rows, split_n, c2)
    shared = lax.all_to_all(partial, "split", split_axis=0, concat_axis=0, tiled=True)
    out = lax.all_to_all(merge(shared, c2), "split", split_axis=0, concat_axis=0, tiled=True)
    return out.astype(jnp.float32).reshape(queries.shape)


def solution(mesh):
    return jax.shard_map(
        local,
        mesh=mesh,
        in_specs=(
            P(None, ("ctx", "split"), None, None),
            P(None, ("ctx", "split"), None, None),
            P(),
            P(),
            P("ctx", None, None, None),
        ),
        out_specs=P("ctx", None, None, None),
        check_vma=False,
    )
```

time: 313 us -> 135 us (0.43)
  blocking collectives: 121 us -> 52 us
  waiting for transfers between devices: 106 us -> 52 us
  matrix products: 42.1 us -> 0 us
  other arithmetic: 16.4 us -> 1.4 us
  between operations: 13.7 us -> 0.12 us
  Pallas kernels: 0 us -> 13.5 us
  starting transfers between devices: 6.23 us -> 11.8 us
    psum x1 -> x0, waiting for transfers between devices: 63.4 us -> none  [local(): lax.psum((total * factor, weighted * factor[:, None]), 'split')]
    dot_general x22 -> x0, matrix products: 42.1 us -> none  [the longest x8 23 us: attend(): jnp.dot(weight.astype(jnp.bfloat16), values_b, preferred_element_type=jnp...]
    all_to_all x3 -> x2, blocking collectives: 89.9 us -> 52 us  [the longest x1 31.6 us: local(): lax.all_to_all(partial, 'split', split_axis=0, concat_axis=0, tiled=True)]
    pmax x1 -> x0, blocking collectives: 19.7 us -> none  [local(): whole_top = lax.pmax(top, 'split')]
    pallas_call x0 -> x3, Pallas kernels: none -> 13.5 us  [the longest x1 8.92 us: attend(): pl.pallas_call(functools.partial(attend_kernel, chunk=chunk, c2=c2), in_s...]
    psum x1 -> x0, blocking collectives: 10.9 us -> none  [local(): lax.psum((total * factor, weighted * factor[:, None]), 'split')]
    reduce_sum x10 -> x1, other arithmetic: 10.4 us -> 0.02 us  [local(): live = jnp.sum(jnp.where(marks, mine, 0), axis=1)]
    all_to_all x1, waiting for transfers between devices: 42.3 us -> 52 us  [local(): lax.all_to_all(message, 'ctx', split_axis=0, concat_axis=0, tiled=True)]
  transfers between devices with their start and end apart: 2 -> 1, of which waited for: 2 -> 1; matrix products, arithmetic and copies ran while one was open for 3% -> 1% of each run, Pallas kernels for 0% -> 0%
where the time goes in v1:
time: 135 us; the launch traced here: 134 us
  waiting for transfers between devices  52 us (39%)
  blocking collectives  52 us (39%)
  Pallas kernels  13.5 us (10%)
  starting transfers between devices  11.8 us (9%)
  local copies, waits for them, and re-layouts  2.99 us (2%)
  other arithmetic  1.4 us (1%)
    all_to_all x1, waiting for transfers between devices, local(): lax.all_to_all(message, 'ctx', split_axis=0, concat_axis=0, tiled=True)  52 us
    all_to_all x1, blocking collectives, local(): lax.all_to_all(partial, 'split', split_axis=0, concat_axis=0, tiled=True)  31.6 us
    all_to_all x1, blocking collectives, local(): lax.all_to_all(merge(shared, c2), 'split', split_axis=0, concat_axis=0, t...  20.4 us
    all_to_all x1, starting transfers between devices, local(): lax.all_to_all(message, 'ctx', split_axis=0, concat_axis=0, tiled=True)  11.8 us
    pallas_call x1, Pallas kernels, attend(): pl.pallas_call(functools.partial(attend_kernel, chunk=chunk, c2=c2), in_s...  8.92 us
    pallas_call x1, Pallas kernels, pack(): pl.pallas_call(pack_kernel, in_specs=[scalars, scalars, pl.BlockSpec(memo...  4.31 us
  transfers between devices with their start and end apart: 1, of which 1 were waited for; matrix products, arithmetic and copies ran while one was open for 1% of the time, Pallas kernels for 0%

profile of v1, /device:TPU:1, one launch (start us, length us, event | category | flops | bytes accessed | tf_op | source)
XLA Modules:
  0.0 133.8 jit_solution(9176759732328928158)
XLA Ops:
  0.0 0.0 copy-start
  0.0 0.8 copy-done
  0.8 0.1 constant_dynamic-slice_fusion
  0.9 0.7 reshape.83.count_ref
  1.6 4.3 %pack.1 = bf16[64,136,128]{2,1,0:T(8,128)(2,1)} custom-call(s32[1]{0:T(128)} %bitcast.2.page_ref, s32[32]{0:T(128)} %reshape.83.count_ref, s32[64,256]{1,0:T(8,128)} %listed_ref.1, bf16[64,2,64,128]{3,2,1,0:T(8,128)(2,1)} %keys_ref.1, bf16[64,2,64,128]{3,2,1,0:T(8,128)(2,1)} %values_ref.1), custom_call_target="tpu_custom_call" | custom-call | tf_op jit(solution)/shard_map/pack/pallas_call | solution.py:78
  5.9 0.0 copy-start.1
  5.9 11.8 %all-to-all-start = ((bf16[64,136,128]{2,1,0:T(8,128)(2,1)}), bf16[64,136,128]{2,1,0:T(8,128)(2,1)S(1)}, u32[]{:S(2)}, u32[]{:S(2)}) async-start(bf16[64,136,128]{2,1,0:T(8,128)(2,1)} %pack.1), calls=%async_computation | async-start | bytes 4456448 | tf_op jit(solution)/shard_map/all_to_all | solution.py:265
  17.7 0.7 constant_dynamic-slice_fusion.2
  18.4 0.2 compare_reduce_fusion
  18.6 0.1 copy.11
  18.7 0.2 reduce_or.12
  18.9 0.2 reshape.81
  19.1 0.1 multiply_reduce_fusion
  19.3 0.1 mul.50
  19.4 0.1 copy.10
  19.5 52.0 %all-to-all-done.got_ref = bf16[64,136,128]{2,1,0:T(8,128)(2,1)S(1)} async-done(((bf16[64,136,128]{2,1,0:T(8,128)(2,1)}), bf16[64,136,128]{2,1,0:T(8,128)(2,1)S(1)}, u32[]{:S(2)}, u32[]{:S(2)}) %all-to-all-start) | async-done | bytes 2228256 | tf_op jit(solution)/shard_map/all_to_all | solution.py:265
  71.5 0.0 copy-done.1
  71.5 8.9 %attend.1 = bf16[8,136,256]{2,1,0:T(8,128)(2,1)S(1)} custom-call(s32[64]{0:T(128)S(1)} %fusion.live_ref, f32[1,128]{1,0:T(1,128)S(1)} %broadcast_select_fusion.cbias_ref, bf16[64,136,128]{2,1,0:T(8,128)(2,1)S(1)} %all-to-all-done.got_ref, bf16[2048,128]{1,0:T(8,128)(2,1)S(1)} %bitcast.9), custom_call_target="tpu_custom_call" | custom-call | flops 4429185024 | bytes 4194304 | tf_op jit(solution)/shard_map/attend/pallas_call | solution.py:200
  80.5 31.6 %all_to_all.15.got_ref = bf16[8,136,256]{2,1,0:T(8,128)(2,1)S(1)} all-to-all(bf16[8,136,256]{2,1,0:T(8,128)(2,1)S(1)} %attend.1), channel_id=1, replica_groups=mesh['ctx'=64,'split'=8] {'split'}, dimensions={0} | all-to-all | bytes 1114112 | tf_op jit(solution)/shard_map/all_to_all | solution.py:280
  112.0 0.2 merge.1
  112.3 20.4 %all_to_all.16 = bf16[8,256,128]{2,1,0:T(8,128)(2,1)S(1)} all-to-all(bf16[8,256,128]{2,1,0:T(8,128)(2,1)S(1)} %merge.1), channel_id=1, replica_groups=mesh['ctx'=64,'split'=8] {'split'}, dimensions={0} | all-to-all | bytes 1048576 | tf_op jit(solution)/shard_map/all_to_all | solution.py:281
  132.7 1.0 convert.1
  (5 shorter events, 0.1 us)
Async XLA Ops:
  0.0 0.8 copy-start
  5.9 65.6 %copy-start.1 = (bf16[1,128,16,128]{3,2,1,0:T(8,128)(2,1)S(1)}, bf16[1,128,16,128]{3,2,1,0:T(8,128)(2,1)}, u32[]{:S(2)}) copy-start(bf16[1,128,16,128]{3,2,1,0:T(8,128)(2,1)} %param.9) | copy-start | bytes 1572868
  5.9 65.6 %all-to-all-start = ((bf16[64,136,128]{2,1,0:T(8,128)(2,1)}), bf16[64,136,128]{2,1,0:T(8,128)(2,1)S(1)}, u32[]{:S(2)}, u32[]{:S(2)}) async-start(bf16[64,136,128]{2,1,0:T(8,128)(2,1)} %pack.1), calls=%async_computation | async-start | bytes 4456448 | tf_op jit(solution)/shard_map/all_to_all | solution.py:265

commit v2 on v1

--- a/solution.py
+++ b/solution.py
@@ -17,8 +17,23 @@
 MiB = 1024 * 1024
 
 
-def pack_kernel(page_ref, count_ref, listed_ref, keys_ref, values_ref, out_ref, cache, message, got, sent):
+def pack_kernel(
+    page_ref,
+    counts_ref,
+    listed_ref,
+    keys_ref,
+    values_ref,
+    out_ref,
+    cache,
+    message,
+    count_here,
+    listed,
+    got,
+    sent,
+    small,
+):
     items = out_ref.shape[0]
+    page = page_ref[0]
     kv_heads = 4
     block = 8
     groups = items // block
@@ -34,12 +49,17 @@
         at = pl.ds(g * block, block)
         return pltpu.make_async_copy(message.at[at], out_ref.at[at], sent.at[g])
 
+    columns = pl.ds(pl.multiple_of((page // HEAD) * HEAD, HEAD), HEAD)
+    lists = pltpu.make_async_copy(listed_ref, listed, small.at[0])
+    numbers = pltpu.make_async_copy(counts_ref.at[:, columns], count_here, small.at[1])
+    lists.start()
+    numbers.start()
     for g in range(groups):
         for copy in fetch(g):
             copy.start()
-    second = jnp.max(
-        jnp.where(listed_ref[...] == page_ref[0] + 1, 1.0, 0.0), axis=1, keepdims=True
-    )
+    lists.wait()
+    second = jnp.max(jnp.where(listed[...] == page + 1, 1.0, 0.0), axis=1, keepdims=True)
+    numbers.wait()
     row = lax.broadcasted_iota(jnp.int32, (16, 4 * PAGE), 0)
     slot = lax.broadcasted_iota(jnp.int32, (16, 4 * PAGE), 1)
     quarter = slot // PAGE
@@ -51,7 +71,7 @@
         for item in range(g * block, (g + 1) * block):
             if item % kv_heads == 0:
                 request = item // kv_heads
-                count = [count_ref[2 * request], count_ref[2 * request + 1]]
+                count = [count_here[request, page % HEAD + p] for p in range(2)]
                 limit = jnp.where(row % 2 == 0, count[0], count[1])
                 live = jnp.logical_and(quarter == row, slot < limit)
                 live = jnp.where(live, 1.0, 0.0).astype(jnp.bfloat16)
@@ -70,25 +90,27 @@
         send(g).wait()
 
 
-def pack(page, local_counts, listed, cache_keys, cache_values):
+def pack(page, counts, listed, cache_keys, cache_values):
     items = cache_keys.shape[0]
     groups = items // 8
     whole = pl.BlockSpec(memory_space=pl.ANY)
-    scalars = pl.BlockSpec(memory_space=pltpu.SMEM)
     return pl.pallas_call(
         pack_kernel,
-        in_specs=[scalars, scalars, pl.BlockSpec(memory_space=pltpu.VMEM), whole, whole],
+        in_specs=[pl.BlockSpec(memory_space=pltpu.SMEM), whole, whole, whole, whole],
         out_specs=whole,
         out_shape=jax.ShapeDtypeStruct((items, ROWS, HEAD), jnp.bfloat16),
         scratch_shapes=[
             pltpu.VMEM((items, 2, 2, PAGE, HEAD), jnp.bfloat16),
             pltpu.VMEM((items, ROWS, HEAD), jnp.bfloat16),
+            pltpu.SMEM((counts.shape[0], HEAD), jnp.int32),
+            pltpu.VMEM(listed.shape, jnp.int32),
             pltpu.SemaphoreType.DMA((2, groups)),
             pltpu.SemaphoreType.DMA((groups,)),
+            pltpu.SemaphoreType.DMA((2,)),
         ],
         compiler_params=pltpu.CompilerParams(vmem_limit_bytes=58 * MiB),
         name="pack",
-    )(page, local_counts, listed, cache_keys, cache_values)
+    )(page, counts, listed, cache_keys, cache_values)
 
 
 def split3(x):
@@ -99,19 +121,19 @@
 
 
 def attend_kernel(
-    live_ref, cbias_ref, got_ref, q_ref, out_ref, ka, vv, vt, qt, sc0, sc1, acc, *, chunk, c2
+    live_ref, cbias_ref, got_ref, q_ref, out_ref, ka, kt, vv, qa, sc0, sc1, best, top, acc, *, chunk, c2
 ):
     sources = got_ref.shape[0]
     cents = 2 * sources
-    block = qt.shape[2]
-    width = out_ref.shape[2]
+    block = qa.shape[1]
+    width = out_ref.shape[1] - 16
     blocks = q_ref.shape[0] // block
     sc = (sc0, sc1)
     lane = lax.broadcasted_iota(jnp.int32, (PAGE, HEAD), 1)
     tok = lax.broadcasted_iota(jnp.int32, (PAGE, HEAD), 0)
-    vt[HEAD:, :] = jnp.ones((vt.shape[0] - HEAD, vt.shape[1]), jnp.bfloat16)
+    vv[:, HEAD:] = jnp.ones((vv.shape[0], HEAD), jnp.bfloat16)
     for i in range(2):
-        qt[i, HEAD:, :] = jnp.ones((HEAD, block), jnp.bfloat16)
+        qa[i, :, HEAD:] = jnp.ones((block, HEAD), jnp.bfloat16)
 
     tails = got_ref[:, 2 * PAGE : ROWS, :].astype(jnp.float32).reshape(sources * TAIL, HEAD)
     tails = tails.astype(jnp.bfloat16)
@@ -132,7 +154,7 @@
         rows = pl.ds(pl.multiple_of(at, 16), PAGE)
         live = live_ref[s]
         ka[rows, :HEAD] = got_ref[s, 0:PAGE, :]
-        vv[rows, :] = got_ref[s, PAGE : 2 * PAGE, :]
+        vv[rows, :HEAD] = got_ref[s, PAGE : 2 * PAGE, :]
         dead = jnp.logical_and(lane == 0, tok >= live)
         ka[rows, HEAD:] = jnp.where(dead, NEG, 0.0).astype(jnp.bfloat16)
         return at + ((live + 15) // 16) * 16
@@ -143,50 +165,57 @@
         rows = pl.ds(pl.multiple_of(end + k, 16), PAGE)
         ka[rows, :HEAD] = jnp.zeros((PAGE, HEAD), jnp.bfloat16)
         ka[rows, HEAD:] = dead
-        vv[rows, :] = jnp.zeros((PAGE, HEAD), jnp.bfloat16)
+        vv[rows, :HEAD] = jnp.zeros((PAGE, HEAD), jnp.bfloat16)
     chunks = (end + chunk - 1) // chunk
 
     def turn(j, carry):
         for k in range(0, chunk, HEAD):
             at = pl.ds(pl.multiple_of(j * chunk + k, HEAD), HEAD)
-            vt[:HEAD, at] = jnp.transpose(vv[at, :].astype(jnp.float32)).astype(jnp.bfloat16)
+            for half in (slice(0, HEAD), slice(HEAD, 2 * HEAD)):
+                kt[half, at] = jnp.transpose(ka[at, half].astype(jnp.float32)).astype(jnp.bfloat16)
         return carry
 
     lax.fori_loop(0, chunks, turn, 0)
 
-    top = None
+    lanes = lax.broadcasted_iota(jnp.int32, (block, HEAD), 1)
     for b in range(blocks + 1):
         if b < blocks:
-            rows = q_ref[b * block : (b + 1) * block, :].astype(jnp.float32)
-            qt[b % 2, :HEAD, :] = jnp.transpose(rows).astype(jnp.bfloat16)
+            qa[b % 2, :, :HEAD] = q_ref[b * block : (b + 1) * block, :]
+            best[...] = jnp.full((block, HEAD), 4 * NEG, jnp.float32)
         if b > 0:
             acc[...] = jnp.zeros_like(acc)
 
-        def body(j, best, b=b, top=top):
+        def body(j, carry, b=b):
             at = pl.ds(pl.multiple_of(j * chunk, chunk), chunk)
             if b > 0:
-                weight = jnp.exp2((sc[(b - 1) % 2][at, :] - top) * c2).astype(jnp.bfloat16)
-                acc[...] += jnp.dot(vt[:, at], weight, preferred_element_type=jnp.float32)
+                tops = jnp.concatenate([top[...]] * (chunk // HEAD), axis=1)
+                weight = jnp.exp2((sc[(b - 1) % 2][:, at] - tops) * c2).astype(jnp.bfloat16)
+                acc[...] += jnp.dot(weight, vv[at, :], preferred_element_type=jnp.float32)
             if b < blocks:
-                score = jnp.dot(ka[at, :], qt[b % 2], preferred_element_type=jnp.float32)
-                sc[b % 2][at, :] = score
-                best = jnp.maximum(best, jnp.max(score.reshape(chunk // 8, 8, block), axis=0))
-            return best
-
-        best = lax.fori_loop(0, chunks, body, jnp.full((8, block), 4 * NEG, jnp.float32))
+                score = jnp.dot(qa[b % 2], kt[:, at], preferred_element_type=jnp.float32)
+                sc[b % 2][:, at] = score
+                parts = [score[:, k : k + HEAD] for k in range(0, chunk, HEAD)]
+                best[...] = functools.reduce(jnp.maximum, parts, best[...])
+            return carry
+
+        lax.fori_loop(0, chunks, body, 0)
         if b > 0:
-            total = acc[HEAD : HEAD + 1, :]
-            out = (acc[:HEAD, :] / total).astype(jnp.bfloat16)
-            row = lax.broadcasted_iota(jnp.int32, (TAIL, block), 0)
-            tile = jnp.zeros((TAIL, block), jnp.float32)
-            for i, piece in enumerate(split3(top) + split3(total)):
-                tile = jnp.where(row == i, piece, tile)
-            tile = tile.astype(jnp.bfloat16)
+            total = acc[:, HEAD:]
+            out = (acc[:, :HEAD] / total).astype(jnp.bfloat16)
+            stats = jnp.transpose(jnp.where(lanes == 0, top[...], total))
+            pieces = split3(stats[0:1, :]) + split3(stats[1:2, :])
+            row = lax.broadcasted_iota(jnp.int32, (16, HEAD), 0)
             for k in range(block // width):
                 to = (b - 1) * (block // width) + k
-                out_ref[to, :HEAD, :] = out[:, k * width : (k + 1) * width]
-                out_ref[to, HEAD:, :] = tile[:, k * width : (k + 1) * width]
-        top = jnp.max(best, axis=0, keepdims=True)
+                out_ref[to, :width, :] = out[k * width : (k + 1) * width, :]
+                tile = jnp.zeros((16, HEAD), jnp.float32)
+                for i, piece in enumerate(pieces):
+                    for h in range(2):
+                        from_ = k * width + h * HEAD
+                        tile = jnp.where(row == 2 * i + h, piece[:, from_ : from_ + HEAD], tile)
+                out_ref[to, width:, :] = tile.astype(jnp.bfloat16)
+        if b < blocks:
+            top[...] = jnp.broadcast_to(jnp.max(best[...], axis=1, keepdims=True), (block, HEAD))
 
 
 def attend(live, cbias, got, rows, parts, c2):
@@ -203,15 +232,17 @@
         out_specs=vmem,
         scratch_shapes=[
             pltpu.VMEM((padded + chunk, 2 * HEAD), jnp.bfloat16),
-            pltpu.VMEM((padded + chunk, HEAD), jnp.bfloat16),
-            pltpu.VMEM((HEAD + 16, padded), jnp.bfloat16),
-            pltpu.VMEM((2, 2 * HEAD, block), jnp.bfloat16),
-            pltpu.VMEM((padded, block), jnp.float32),
-            pltpu.VMEM((padded, block), jnp.float32),
-            pltpu.VMEM((HEAD + 16, block), jnp.float32),
+            pltpu.VMEM((2 * HEAD, padded), jnp.bfloat16),
+            pltpu.VMEM((padded + chunk, 2 * HEAD), jnp.bfloat16),
+            pltpu.VMEM((2, block, 2 * HEAD), jnp.bfloat16),
+            pltpu.VMEM((block, padded), jnp.float32),
+            pltpu.VMEM((block, padded), jnp.float32),
+            pltpu.VMEM((block, HEAD), jnp.float32),
+            pltpu.VMEM((block, HEAD), jnp.float32),
+            pltpu.VMEM((block, 2 * HEAD), jnp.float32),
         ],
-        out_shape=jax.ShapeDtypeStruct((parts, HEAD + TAIL, width), jnp.bfloat16),
-        compiler_params=pltpu.CompilerParams(vmem_limit_bytes=36 * MiB),
+        out_shape=jax.ShapeDtypeStruct((parts, width + 16, HEAD), jnp.bfloat16),
+        compiler_params=pltpu.CompilerParams(vmem_limit_bytes=40 * MiB),
         cost_estimate=pl.CostEstimate(
             flops=4 * rows.shape[0] * keys * HEAD,
             bytes_accessed=4 * MiB,
@@ -223,24 +254,30 @@
 
 def merge_kernel(got_ref, out_ref, *, c2):
     parts = got_ref.shape[0]
+    block = out_ref.shape[1]
     tops, totals = [], []
     for z in range(parts):
-        tile = got_ref[z, HEAD:, :].astype(jnp.float32)
-        tops.append(tile[0:1] + tile[1:2] + tile[2:3])
-        totals.append(tile[3:4] + tile[4:5] + tile[5:6])
+        tile = got_ref[z, block:, :].astype(jnp.float32)
+        tops.append(tile[0:2] + tile[2:4] + tile[4:6])
+        totals.append(tile[6:8] + tile[8:10] + tile[10:12])
     top = functools.reduce(jnp.maximum, tops)
     factors = [t * jnp.exp2((m - top) * c2) for m, t in zip(tops, totals)]
     whole = functools.reduce(jnp.add, factors)
-    out = jnp.zeros(got_ref.shape[1:], jnp.float32)[:HEAD]
-    for z in range(parts):
-        out += got_ref[z, :HEAD, :].astype(jnp.float32) * (factors[z] / whole)
-    out = jnp.transpose(out).astype(jnp.bfloat16)
-    for z in range(parts):
-        out_ref[z] = out
+    columns = jnp.transpose(jnp.concatenate([f / whole for f in factors], axis=0))
+    for h in range(2):
+        at = slice(h * HEAD, (h + 1) * HEAD)
+        out = jnp.zeros((HEAD, HEAD), jnp.float32)
+        for z in range(parts):
+            column = columns[:, 2 * z + h : 2 * z + h + 1]
+            out += got_ref[z, at, :].astype(jnp.float32) * column
+        out = out.astype(jnp.bfloat16)
+        for z in range(parts):
+            out_ref[z, at, :] = out
 
 
 def merge(got, c2):
-    parts, unused, block = got.shape
+    parts, block, unused = got.shape
+    block -= 16
     return pl.pallas_call(
         functools.partial(merge_kernel, c2=c2),
         out_shape=jax.ShapeDtypeStruct((parts, block, HEAD), jnp.bfloat16),
@@ -260,8 +297,7 @@
     item = lax.axis_index("ctx")
     split_idx = lax.axis_index("split")
     first = (item * split_n + split_idx) * pages_here
-    local_counts = lax.dynamic_slice_in_dim(counts, first, pages_here, 1).reshape(-1)
-    message = pack(first.reshape(1), local_counts, listed, cache_keys, cache_values)
+    message = pack(first.reshape(1), counts, listed, cache_keys, cache_values)
     got = lax.all_to_all(message, "ctx", split_axis=0, concat_axis=0, tiled=True)
 
     sel_row = lax.dynamic_index_in_dim(listed, item, 0, keepdims=False)

time: 135 us -> 136 us (level)
  the two profiles are of different devices: /device:TPU:1 before, /device:TPU:3 now
where the time goes in v2:
time: 136 us; the launch traced here: 135 us
  blocking collectives  54.9 us (40%)
  waiting for transfers between devices  51.1 us (38%)
  Pallas kernels  14.4 us (11%)
  starting transfers between devices  11.1 us (8%)
  local copies, waits for them, and re-layouts  2.17 us (2%)
  other arithmetic  1.4 us (1%)
    all_to_all x1, waiting for transfers between devices, local(): lax.all_to_all(message, 'ctx', split_axis=0, concat_axis=0, tiled=True)  51.1 us
    all_to_all x1, blocking collectives, local(): lax.all_to_all(partial, 'split', split_axis=0, concat_axis=0, tiled=True)  34.5 us
    all_to_all x1, blocking collectives, local(): lax.all_to_all(merge(shared, c2), 'split', split_axis=0, concat_axis=0, t...  20.4 us
    all_to_all x1, starting transfers between devices, local(): lax.all_to_all(message, 'ctx', split_axis=0, concat_axis=0, tiled=True)  11.1 us
    pallas_call x1, Pallas kernels, attend(): pl.pallas_call(functools.partial(attend_kernel, chunk=chunk, c2=c2), in_s...  9.35 us
    pallas_call x1, Pallas kernels, pack(): pl.pallas_call(pack_kernel, in_specs=[pl.BlockSpec(memory_space=pltpu.SME...  4.48 us
  transfers between devices with their start and end apart: 1, of which 1 were waited for; matrix products, arithmetic and copies ran while one was open for 2% of the time, Pallas kernels for 0%

profile of v2, /device:TPU:3, one launch (start us, length us, event | category | flops | bytes accessed | tf_op | source)
XLA Modules:
  0.0 135.1 jit_solution(3807283660801636456)
XLA Ops:
  0.0 4.5 %pack.1 = bf16[64,136,128]{2,1,0:T(8,128)(2,1)} custom-call(s32[1]{0:T(128)} %bitcast.2.page_ref, s32[16,1024]{1,0:T(8,128)} %counts_ref.1, s32[64,256]{1,0:T(8,128)} %listed_ref.1, bf16[64,2,64,128]{3,2,1,0:T(8,128)(2,1)} %keys_ref.1, bf16[64,2,64,128]{3,2,1,0:T(8,128)(2,1)} %values_ref.1), custom_call_target="tpu_custom_call" | custom-call | tf_op jit(solution)/shard_map/pack/pallas_call | solution.py:97
  4.5 0.0 copy-start
  4.5 11.1 %all-to-all-start = ((bf16[64,136,128]{2,1,0:T(8,128)(2,1)}), bf16[64,136,128]{2,1,0:T(8,128)(2,1)S(1)}, u32[]{:S(2)}, u32[]{:S(2)}) async-start(bf16[64,136,128]{2,1,0:T(8,128)(2,1)} %pack.1), calls=%async_computation | async-start | bytes 4456448 | tf_op jit(solution)/shard_map/all_to_all | solution.py:301
  15.7 0.7 constant_dynamic-slice_fusion.1
  16.4 0.2 compare_reduce_fusion
  16.6 0.1 copy.11
  16.7 0.2 reduce_or.12
  16.8 0.8 dynamic-slice_reduce_fusion
  17.6 0.2 reshape.78
  17.8 0.1 multiply_reduce_fusion
  18.0 0.1 mul.50
  18.1 0.1 copy.10
  18.2 51.1 %all-to-all-done.got_ref = bf16[64,136,128]{2,1,0:T(8,128)(2,1)S(1)} async-done(((bf16[64,136,128]{2,1,0:T(8,128)(2,1)}), bf16[64,136,128]{2,1,0:T(8,128)(2,1)S(1)}, u32[]{:S(2)}, u32[]{:S(2)}) %all-to-all-start) | async-done | bytes 2228256 | tf_op jit(solution)/shard_map/all_to_all | solution.py:301
  69.3 0.0 copy-done
  69.3 9.3 %attend.1 = bf16[8,272,128]{2,1,0:T(8,128)(2,1)S(1)} custom-call(s32[64]{0:T(128)S(1)} %fusion.live_ref, f32[1,128]{1,0:T(1,128)S(1)} %broadcast_select_fusion.cbias_ref, bf16[64,136,128]{2,1,0:T(8,128)(2,1)S(1)} %all-to-all-done.got_ref, bf16[2048,128]{1,0:T(8,128)(2,1)S(1)} %bitcast.9), custom_call_target="tpu_custom_call" | custom-call | flops 4429185024 | bytes 4194304 | tf_op jit(solution)/shard_map/attend/pallas_call | solution.py:229
  78.7 34.5 %all_to_all.15.got_ref = bf16[8,272,128]{2,1,0:T(8,128)(2,1)S(1)} all-to-all(bf16[8,272,128]{2,1,0:T(8,128)(2,1)S(1)} %attend.1), channel_id=1, replica_groups=mesh['ctx'=64,'split'=8] {'split'}, dimensions={0} | all-to-all | bytes 1114112 | tf_op jit(solution)/shard_map/all_to_all | solution.py:316
  113.2 0.5 merge.1
  113.7 20.4 %all_to_all.16 = bf16[8,256,128]{2,1,0:T(8,128)(2,1)S(1)} all-to-all(bf16[8,256,128]{2,1,0:T(8,128)(2,1)S(1)} %merge.1), channel_id=1, replica_groups=mesh['ctx'=64,'split'=8] {'split'}, dimensions={0} | all-to-all | bytes 1048576 | tf_op jit(solution)/shard_map/all_to_all | solution.py:317
  134.1 1.0 convert.1
  (4 shorter events, 0.0 us)
Async XLA Ops:
  4.5 64.8 %copy-start = (bf16[1,128,16,128]{3,2,1,0:T(8,128)(2,1)S(1)}, bf16[1,128,16,128]{3,2,1,0:T(8,128)(2,1)}, u32[]{:S(2)}) copy-start(bf16[1,128,16,128]{3,2,1,0:T(8,128)(2,1)} %param.9) | copy-start | bytes 1572868
  4.5 64.8 %all-to-all-start = ((bf16[64,136,128]{2,1,0:T(8,128)(2,1)}), bf16[64,136,128]{2,1,0:T(8,128)(2,1)S(1)}, u32[]{:S(2)}, u32[]{:S(2)}) async-start(bf16[64,136,128]{2,1,0:T(8,128)(2,1)} %pack.1), calls=%async_computation | async-start | bytes 4456448 | tf_op jit(solution)/shard_map/all_to_all | solution.py:301

commit v3 on v2

--- a/solution.py
+++ b/solution.py
@@ -8,7 +8,6 @@
 from jax.sharding import PartitionSpec as P
 
 NEG = -1e30
-LOG2E = 1.4426950408889634
 
 PAGE = 64
 HEAD = 128
@@ -121,58 +120,72 @@
 
 
 def attend_kernel(
-    live_ref, cbias_ref, got_ref, q_ref, out_ref, ka, kt, vv, qa, sc0, sc1, best, top, acc, *, chunk, c2
+    live_ref,
+    cbias_ref,
+    got_ref,
+    q_ref,
+    out_ref,
+    keys,
+    values,
+    kt,
+    vv,
+    ckt,
+    cv,
+    cs0,
+    cs1,
+    sc0,
+    sc1,
+    best,
+    top,
+    acc,
+    *,
+    chunk,
+    block,
+    c,
 ):
     sources = got_ref.shape[0]
     cents = 2 * sources
-    block = qa.shape[1]
     width = out_ref.shape[1] - 16
     blocks = q_ref.shape[0] // block
-    sc = (sc0, sc1)
-    lane = lax.broadcasted_iota(jnp.int32, (PAGE, HEAD), 1)
-    tok = lax.broadcasted_iota(jnp.int32, (PAGE, HEAD), 0)
-    vv[:, HEAD:] = jnp.ones((vv.shape[0], HEAD), jnp.bfloat16)
-    for i in range(2):
-        qa[i, :, HEAD:] = jnp.ones((block, HEAD), jnp.bfloat16)
+    sc, cs = (sc0, sc1), (cs0, cs1)
 
     tails = got_ref[:, 2 * PAGE : ROWS, :].astype(jnp.float32).reshape(sources * TAIL, HEAD)
     tails = tails.astype(jnp.bfloat16)
     r = lax.broadcasted_iota(jnp.int32, (cents, sources * TAIL), 0)
-    c = lax.broadcasted_iota(jnp.int32, (cents, sources * TAIL), 1)
+    col = lax.broadcasted_iota(jnp.int32, (cents, sources * TAIL), 1)
     first = (r // 2) * TAIL + r % 2
-    for off, ref in ((0, ka), (2, vv)):
-        chosen = (c == first + off).astype(jnp.float32).astype(jnp.bfloat16)
-        ref[0:cents, :HEAD] = jnp.dot(
-            chosen, tails, preferred_element_type=jnp.float32
-        ).astype(jnp.bfloat16)
-    high, middle, low = split3(jnp.transpose(jnp.broadcast_to(cbias_ref[...], (cents, cents))))
-    clane = lax.broadcasted_iota(jnp.int32, (cents, HEAD), 1)
-    bias = jnp.where(clane == 0, high, jnp.where(clane == 1, middle, low))
-    ka[0:cents, HEAD:] = jnp.where(clane < 3, bias, 0.0).astype(jnp.bfloat16)
+    cents_of = [
+        jnp.dot(
+            (col == first + off).astype(jnp.float32).astype(jnp.bfloat16),
+            tails,
+            preferred_element_type=jnp.float32,
+        )
+        for off in (0, 2)
+    ]
+    ckt[...] = jnp.transpose(cents_of[0]).astype(jnp.bfloat16)
+    cv[:, :HEAD] = cents_of[1].astype(jnp.bfloat16)
+    cv[:, HEAD:] = jnp.ones((cents, HEAD), jnp.bfloat16)
 
     def place(s, at):
-        rows = pl.ds(pl.multiple_of(at, 16), PAGE)
-        live = live_ref[s]
-        ka[rows, :HEAD] = got_ref[s, 0:PAGE, :]
-        vv[rows, :HEAD] = got_ref[s, PAGE : 2 * PAGE, :]
-        dead = jnp.logical_and(lane == 0, tok >= live)
-        ka[rows, HEAD:] = jnp.where(dead, NEG, 0.0).astype(jnp.bfloat16)
-        return at + ((live + 15) // 16) * 16
-
-    end = lax.fori_loop(0, sources, place, cents)
-    dead = jnp.where(lane == 0, NEG, 0.0).astype(jnp.bfloat16)
-    for k in range(0, chunk, PAGE):
-        rows = pl.ds(pl.multiple_of(end + k, 16), PAGE)
-        ka[rows, :HEAD] = jnp.zeros((PAGE, HEAD), jnp.bfloat16)
-        ka[rows, HEAD:] = dead
-        vv[rows, :HEAD] = jnp.zeros((PAGE, HEAD), jnp.bfloat16)
+        rows = pl.ds(at, PAGE)
+        keys[rows, :] = got_ref[s, 0:PAGE, :].astype(jnp.float32)
+        values[rows, :] = got_ref[s, PAGE : 2 * PAGE, :].astype(jnp.float32)
+        return at + live_ref[s]
+
+    end = lax.fori_loop(0, sources, place, 0, unroll=4)
     chunks = (end + chunk - 1) // chunk
+    rest = pl.ds(end, chunk)
+    keys[rest, :] = jnp.broadcast_to(keys[0:1, :], (chunk, HEAD))
+    values[rest, :] = jnp.zeros((chunk, HEAD), jnp.float32)
+    number = lax.broadcasted_iota(jnp.int32, (HEAD, HEAD), 0)
 
     def turn(j, carry):
         for k in range(0, chunk, HEAD):
-            at = pl.ds(pl.multiple_of(j * chunk + k, HEAD), HEAD)
-            for half in (slice(0, HEAD), slice(HEAD, 2 * HEAD)):
-                kt[half, at] = jnp.transpose(ka[at, half].astype(jnp.float32)).astype(jnp.bfloat16)
+            start = pl.multiple_of(j * chunk + k, HEAD)
+            at = pl.ds(start, HEAD)
+            kt[:, at] = jnp.transpose(keys[at, :]).astype(jnp.bfloat16)
+            vv[at, :HEAD] = values[at, :].astype(jnp.bfloat16)
+            vv[at, HEAD:] = jnp.where(number + start < end, 1.0, 0.0).astype(jnp.bfloat16)
         return carry
 
     lax.fori_loop(0, chunks, turn, 0)
@@ -180,22 +193,33 @@
     lanes = lax.broadcasted_iota(jnp.int32, (block, HEAD), 1)
     for b in range(blocks + 1):
         if b < blocks:
-            qa[b % 2, :, :HEAD] = q_ref[b * block : (b + 1) * block, :]
-            best[...] = jnp.full((block, HEAD), 4 * NEG, jnp.float32)
+            rows = q_ref[b * block : (b + 1) * block, :]
+            score = jnp.dot(rows, ckt[...], preferred_element_type=jnp.float32) + cbias_ref[...]
+            cs[b % 2][...] = score
+            best[...] = score
         if b > 0:
-            acc[...] = jnp.zeros_like(acc)
+            weight = jnp.exp((cs[(b - 1) % 2][...] - top[...]) * c).astype(jnp.bfloat16)
+            acc[...] = jnp.dot(weight, cv[...], preferred_element_type=jnp.float32)
 
         def body(j, carry, b=b):
             at = pl.ds(pl.multiple_of(j * chunk, chunk), chunk)
             if b > 0:
                 tops = jnp.concatenate([top[...]] * (chunk // HEAD), axis=1)
-                weight = jnp.exp2((sc[(b - 1) % 2][:, at] - tops) * c2).astype(jnp.bfloat16)
-                acc[...] += jnp.dot(weight, vv[at, :], preferred_element_type=jnp.float32)
+                weight = jnp.exp((sc[(b - 1) % 2][:, at] - tops) * c).astype(jnp.bfloat16)
+                half = chunk // 2
+                for k in range(2):
+                    at_k = pl.ds(pl.multiple_of(j * chunk + k * half, half), half)
+                    acc[...] += jnp.dot(
+                        weight[:, k * half : (k + 1) * half],
+                        vv[at_k, :],
+                        preferred_element_type=jnp.float32,
+                    )
             if b < blocks:
-                score = jnp.dot(qa[b % 2], kt[:, at], preferred_element_type=jnp.float32)
+                rows = q_ref[b * block : (b + 1) * block, :]
+                score = jnp.dot(rows, kt[:, at], preferred_element_type=jnp.float32)
                 sc[b % 2][:, at] = score
                 parts = [score[:, k : k + HEAD] for k in range(0, chunk, HEAD)]
-                best[...] = functools.reduce(jnp.maximum, parts, best[...])
+                best[...] = jnp.maximum(best[...], functools.reduce(jnp.maximum, parts))
             return carry
 
         lax.fori_loop(0, chunks, body, 0)
@@ -218,25 +242,29 @@
             top[...] = jnp.broadcast_to(jnp.max(best[...], axis=1, keepdims=True), (block, HEAD))
 
 
-def attend(live, cbias, got, rows, parts, c2):
+def attend(live, cbias, got, rows, parts, c):
     sources = got.shape[0]
     chunk = 512
     block = 512
-    keys = sources * (PAGE + 2)
-    padded = pl.cdiv(keys, chunk) * chunk
+    slots = sources * PAGE
+    cents = 2 * sources
     width = rows.shape[0] // parts
     vmem = pl.BlockSpec(memory_space=pltpu.VMEM)
     return pl.pallas_call(
-        functools.partial(attend_kernel, chunk=chunk, c2=c2),
+        functools.partial(attend_kernel, chunk=chunk, block=block, c=c),
         in_specs=[pl.BlockSpec(memory_space=pltpu.SMEM), vmem, vmem, vmem],
         out_specs=vmem,
         scratch_shapes=[
-            pltpu.VMEM((padded + chunk, 2 * HEAD), jnp.bfloat16),
-            pltpu.VMEM((2 * HEAD, padded), jnp.bfloat16),
-            pltpu.VMEM((padded + chunk, 2 * HEAD), jnp.bfloat16),
-            pltpu.VMEM((2, block, 2 * HEAD), jnp.bfloat16),
-            pltpu.VMEM((block, padded), jnp.float32),
-            pltpu.VMEM((block, padded), jnp.float32),
+            pltpu.VMEM((slots + chunk, HEAD), jnp.float32),
+            pltpu.VMEM((slots + chunk, HEAD), jnp.float32),
+            pltpu.VMEM((HEAD, slots), jnp.bfloat16),
+            pltpu.VMEM((slots, 2 * HEAD), jnp.bfloat16),
+            pltpu.VMEM((HEAD, cents), jnp.bfloat16),
+            pltpu.VMEM((cents, 2 * HEAD), jnp.bfloat16),
+            pltpu.VMEM((block, cents), jnp.float32),
+            pltpu.VMEM((block, cents), jnp.float32),
+            pltpu.VMEM((block, slots), jnp.float32),
+            pltpu.VMEM((block, slots), jnp.float32),
             pltpu.VMEM((block, HEAD), jnp.float32),
             pltpu.VMEM((block, HEAD), jnp.float32),
             pltpu.VMEM((block, 2 * HEAD), jnp.float32),
@@ -244,15 +272,15 @@
         out_shape=jax.ShapeDtypeStruct((parts, width + 16, HEAD), jnp.bfloat16),
         compiler_params=pltpu.CompilerParams(vmem_limit_bytes=40 * MiB),
         cost_estimate=pl.CostEstimate(
-            flops=4 * rows.shape[0] * keys * HEAD,
+            flops=4 * rows.shape[0] * (slots + cents) * HEAD,
             bytes_accessed=4 * MiB,
-            transcendentals=rows.shape[0] * keys,
+            transcendentals=rows.shape[0] * (slots + cents),
         ),
         name="attend",
     )(live, cbias, got, rows)
 
 
-def merge_kernel(got_ref, out_ref, *, c2):
+def merge_kernel(got_ref, out_ref, *, c):
     parts = got_ref.shape[0]
     block = out_ref.shape[1]
     tops, totals = [], []
@@ -261,7 +289,7 @@
         tops.append(tile[0:2] + tile[2:4] + tile[4:6])
         totals.append(tile[6:8] + tile[8:10] + tile[10:12])
     top = functools.reduce(jnp.maximum, tops)
-    factors = [t * jnp.exp2((m - top) * c2) for m, t in zip(tops, totals)]
+    factors = [t * jnp.exp((m - top) * c) for m, t in zip(tops, totals)]
     whole = functools.reduce(jnp.add, factors)
     columns = jnp.transpose(jnp.concatenate([f / whole for f in factors], axis=0))
     for h in range(2):
@@ -275,11 +303,11 @@
             out_ref[z, at, :] = out
 
 
-def merge(got, c2):
+def merge(got, c):
     parts, block, unused = got.shape
     block -= 16
     return pl.pallas_call(
-        functools.partial(merge_kernel, c2=c2),
+        functools.partial(merge_kernel, c=c),
         out_shape=jax.ShapeDtypeStruct((parts, block, HEAD), jnp.bfloat16),
         compiler_params=pltpu.CompilerParams(vmem_limit_bytes=16 * MiB),
         name="merge",
@@ -293,7 +321,7 @@
     requests = counts.shape[0]
     kv_heads = items // requests
     root = head**0.5
-    c2 = head**-0.5 * LOG2E
+    c = head**-0.5
     item = lax.axis_index("ctx")
     split_idx = lax.axis_index("split")
     first = (item * split_n + split_idx) * pages_here
@@ -312,9 +340,9 @@
     live = jnp.sum(jnp.where(marks, mine, 0), axis=1)
     cbias = jnp.where(marks, NEG, jnp.log(mine.astype(jnp.float32)) * root)
     rows = queries.reshape(-1, head)
-    partial = attend(live, cbias.reshape(1, -1), got, rows, split_n, c2)
+    partial = attend(live, cbias.reshape(1, -1), got, rows, split_n, c)
     shared = lax.all_to_all(partial, "split", split_axis=0, concat_axis=0, tiled=True)
-    out = lax.all_to_all(merge(shared, c2), "split", split_axis=0, concat_axis=0, tiled=True)
+    out = lax.all_to_all(merge(shared, c), "split", split_axis=0, concat_axis=0, tiled=True)
     return out.astype(jnp.float32).reshape(queries.shape)
 
 

time: 136 us -> 132 us (0.971)
  the two profiles are of different devices: /device:TPU:3 before, /device:TPU:7 now
where the time goes in v3:
time: 132 us
  blocking collectives  53.8 us (41%)
  waiting for transfers between devices  51.1 us (39%)
  Pallas kernels  11.8 us (9%)
  starting transfers between devices  11.3 us (9%)
  local copies, waits for them, and re-layouts  2.17 us (2%)
  other arithmetic  1.4 us (1%)
    all_to_all x1, waiting for transfers between devices, local(): lax.all_to_all(message, 'ctx', split_axis=0, concat_axis=0, tiled=True)  51.1 us
    all_to_all x1, blocking collectives, local(): lax.all_to_all(partial, 'split', split_axis=0, concat_axis=0, tiled=True)  33.3 us
    all_to_all x1, blocking collectives, local(): lax.all_to_all(merge(shared, c), 'split', split_axis=0, concat_axis=0, ti...  20.4 us
    all_to_all x1, starting transfers between devices, local(): lax.all_to_all(message, 'ctx', split_axis=0, concat_axis=0, tiled=True)  11.3 us
    pallas_call x1, Pallas kernels, attend(): pl.pallas_call(functools.partial(attend_kernel, chunk=chunk, block=block,...  6.76 us
    pallas_call x1, Pallas kernels, pack(): pl.pallas_call(pack_kernel, in_specs=[pl.BlockSpec(memory_space=pltpu.SME...  4.48 us
  transfers between devices with their start and end apart: 1, of which 1 were waited for; matrix products, arithmetic and copies ran while one was open for 2% of the time, Pallas kernels for 0%

profile of v3, /device:TPU:7, one launch (start us, length us, event | category | flops | bytes accessed | tf_op | source)
XLA Modules:
  0.0 131.6 jit_solution(1988231561074488381)
XLA Ops:
  0.0 4.5 %pack.1 = bf16[64,136,128]{2,1,0:T(8,128)(2,1)} custom-call(s32[1]{0:T(128)} %bitcast.2.page_ref, s32[16,1024]{1,0:T(8,128)} %counts_ref.1, s32[64,256]{1,0:T(8,128)} %listed_ref.1, bf16[64,2,64,128]{3,2,1,0:T(8,128)(2,1)} %keys_ref.1, bf16[64,2,64,128]{3,2,1,0:T(8,128)(2,1)} %values_ref.1), custom_call_target="tpu_custom_call" | custom-call | tf_op jit(solution)/shard_map/pack/pallas_call | solution.py:96
  4.5 0.0 copy-start
  4.5 11.3 %all-to-all-start = ((bf16[64,136,128]{2,1,0:T(8,128)(2,1)}), bf16[64,136,128]{2,1,0:T(8,128)(2,1)S(1)}, u32[]{:S(2)}, u32[]{:S(2)}) async-start(bf16[64,136,128]{2,1,0:T(8,128)(2,1)} %pack.1), calls=%async_computation | async-start | bytes 4456448 | tf_op jit(solution)/shard_map/all_to_all | solution.py:329
  15.8 0.7 constant_dynamic-slice_fusion.1
  16.5 0.2 compare_reduce_fusion
  16.7 0.1 copy.11
  16.8 0.2 reduce_or.12
  17.0 0.8 dynamic-slice_reduce_fusion
  17.8 0.2 reshape.78
  18.0 0.1 multiply_reduce_fusion
  18.1 0.1 mul.50
  18.2 0.1 copy.10
  18.4 51.1 %all-to-all-done.got_ref = bf16[64,136,128]{2,1,0:T(8,128)(2,1)S(1)} async-done(((bf16[64,136,128]{2,1,0:T(8,128)(2,1)}), bf16[64,136,128]{2,1,0:T(8,128)(2,1)S(1)}, u32[]{:S(2)}, u32[]{:S(2)}) %all-to-all-start) | async-done | bytes 2228256 | tf_op jit(solution)/shard_map/all_to_all | solution.py:329
  69.5 0.0 copy-done
  69.5 6.8 %attend.1 = bf16[8,272,128]{2,1,0:T(8,128)(2,1)S(1)} custom-call(s32[64]{0:T(128)S(1)} %fusion.live_ref, f32[1,128]{1,0:T(1,128)S(1)} %broadcast_select_fusion.cbias_ref, bf16[64,136,128]{2,1,0:T(8,128)(2,1)S(1)} %all-to-all-done.got_ref, bf16[2048,128]{1,0:T(8,128)(2,1)S(1)} %bitcast.9), custom_call_target="tpu_custom_call" | custom-call | flops 4429185024 | bytes 4194304 | tf_op jit(solution)/shard_map/attend/pallas_call | solution.py:253
  76.2 33.3 %all_to_all.15.got_ref = bf16[8,272,128]{2,1,0:T(8,128)(2,1)S(1)} all-to-all(bf16[8,272,128]{2,1,0:T(8,128)(2,1)S(1)} %attend.1), channel_id=1, replica_groups=mesh['ctx'=64,'split'=8] {'split'}, dimensions={0} | all-to-all | bytes 1114112 | tf_op jit(solution)/shard_map/all_to_all | solution.py:344
  109.6 0.5 merge.1
  110.1 20.4 %all_to_all.16 = bf16[8,256,128]{2,1,0:T(8,128)(2,1)S(1)} all-to-all(bf16[8,256,128]{2,1,0:T(8,128)(2,1)S(1)} %merge.1), channel_id=1, replica_groups=mesh['ctx'=64,'split'=8] {'split'}, dimensions={0} | all-to-all | bytes 1048576 | tf_op jit(solution)/shard_map/all_to_all | solution.py:345
  130.5 1.0 convert.1
  (4 shorter events, 0.0 us)
Async XLA Ops:
  4.5 65.0 %copy-start = (bf16[1,128,16,128]{3,2,1,0:T(8,128)(2,1)S(1)}, bf16[1,128,16,128]{3,2,1,0:T(8,128)(2,1)}, u32[]{:S(2)}) copy-start(bf16[1,128,16,128]{3,2,1,0:T(8,128)(2,1)} %param.9) | copy-start | bytes 1572868
  4.5 65.0 %all-to-all-start = ((bf16[64,136,128]{2,1,0:T(8,128)(2,1)}), bf16[64,136,128]{2,1,0:T(8,128)(2,1)S(1)}, u32[]{:S(2)}, u32[]{:S(2)}) async-start(bf16[64,136,128]{2,1,0:T(8,128)(2,1)} %pack.1), calls=%async_computation | async-start | bytes 4456448 | tf_op jit(solution)/shard_map/all_to_all | solution.py:329

commit v4 on v3

--- a/solution.py
+++ b/solution.py
@@ -8,6 +8,7 @@
 from jax.sharding import PartitionSpec as P
 
 NEG = -1e30
+LOG2E = 1.4426950408889634
 
 PAGE = 64
 HEAD = 128
@@ -119,6 +120,12 @@
     return high, middle, rest - middle
 
 
+def store_scaled(ref, at, x):
+    high = x.astype(jnp.bfloat16)
+    ref[:HEAD, at] = high
+    ref[HEAD:, at] = (x - high.astype(jnp.float32)).astype(jnp.bfloat16)
+
+
 def attend_kernel(
     live_ref,
     cbias_ref,
@@ -131,6 +138,7 @@
     vv,
     ckt,
     cv,
+    qq,
     cs0,
     cs1,
     sc0,
@@ -162,7 +170,7 @@
         )
         for off in (0, 2)
     ]
-    ckt[...] = jnp.transpose(cents_of[0]).astype(jnp.bfloat16)
+    store_scaled(ckt, slice(None), jnp.transpose(cents_of[0].astype(jnp.bfloat16).astype(jnp.float32)) * c)
     cv[:, :HEAD] = cents_of[1].astype(jnp.bfloat16)
     cv[:, HEAD:] = jnp.ones((cents, HEAD), jnp.bfloat16)
 
@@ -183,7 +191,7 @@
         for k in range(0, chunk, HEAD):
             start = pl.multiple_of(j * chunk + k, HEAD)
             at = pl.ds(start, HEAD)
-            kt[:, at] = jnp.transpose(keys[at, :]).astype(jnp.bfloat16)
+            store_scaled(kt, at, jnp.transpose(keys[at, :]) * c)
             vv[at, :HEAD] = values[at, :].astype(jnp.bfloat16)
             vv[at, HEAD:] = jnp.where(number + start < end, 1.0, 0.0).astype(jnp.bfloat16)
         return carry
@@ -194,29 +202,23 @@
     for b in range(blocks + 1):
         if b < blocks:
             rows = q_ref[b * block : (b + 1) * block, :]
-            score = jnp.dot(rows, ckt[...], preferred_element_type=jnp.float32) + cbias_ref[...]
+            qq[:, :HEAD] = rows
+            qq[:, HEAD:] = rows
+            score = jnp.dot(qq[...], ckt[...], preferred_element_type=jnp.float32) + cbias_ref[...]
             cs[b % 2][...] = score
             best[...] = score
         if b > 0:
-            weight = jnp.exp((cs[(b - 1) % 2][...] - top[...]) * c).astype(jnp.bfloat16)
+            weight = jnp.exp2(cs[(b - 1) % 2][...] - top[...]).astype(jnp.bfloat16)
             acc[...] = jnp.dot(weight, cv[...], preferred_element_type=jnp.float32)
 
         def body(j, carry, b=b):
             at = pl.ds(pl.multiple_of(j * chunk, chunk), chunk)
             if b > 0:
                 tops = jnp.concatenate([top[...]] * (chunk // HEAD), axis=1)
-                weight = jnp.exp((sc[(b - 1) % 2][:, at] - tops) * c).astype(jnp.bfloat16)
-                half = chunk // 2
-                for k in range(2):
-                    at_k = pl.ds(pl.multiple_of(j * chunk + k * half, half), half)
-                    acc[...] += jnp.dot(
-                        weight[:, k * half : (k + 1) * half],
-                        vv[at_k, :],
-                        preferred_element_type=jnp.float32,
-                    )
+                weight = jnp.exp2(sc[(b - 1) % 2][:, at] - tops).astype(jnp.bfloat16)
+                acc[...] += jnp.dot(weight, vv[at, :], preferred_element_type=jnp.float32)
             if b < blocks:
-                rows = q_ref[b * block : (b + 1) * block, :]
-                score = jnp.dot(rows, kt[:, at], preferred_element_type=jnp.float32)
+                score = jnp.dot(qq[...], kt[:, at], preferred_element_type=jnp.float32)
                 sc[b % 2][:, at] = score
                 parts = [score[:, k : k + HEAD] for k in range(0, chunk, HEAD)]
                 best[...] = jnp.maximum(best[...], functools.reduce(jnp.maximum, parts))
@@ -257,10 +259,11 @@
         scratch_shapes=[
             pltpu.VMEM((slots + chunk, HEAD), jnp.float32),
             pltpu.VMEM((slots + chunk, HEAD), jnp.float32),
-            pltpu.VMEM((HEAD, slots), jnp.bfloat16),
+            pltpu.VMEM((2 * HEAD, slots), jnp.bfloat16),
             pltpu.VMEM((slots, 2 * HEAD), jnp.bfloat16),
-            pltpu.VMEM((HEAD, cents), jnp.bfloat16),
+            pltpu.VMEM((2 * HEAD, cents), jnp.bfloat16),
             pltpu.VMEM((cents, 2 * HEAD), jnp.bfloat16),
+            pltpu.VMEM((block, 2 * HEAD), jnp.bfloat16),
             pltpu.VMEM((block, cents), jnp.float32),
             pltpu.VMEM((block, cents), jnp.float32),
             pltpu.VMEM((block, slots), jnp.float32),
@@ -280,7 +283,7 @@
     )(live, cbias, got, rows)
 
 
-def merge_kernel(got_ref, out_ref, *, c):
+def merge_kernel(got_ref, out_ref):
     parts = got_ref.shape[0]
     block = out_ref.shape[1]
     tops, totals = [], []
@@ -289,7 +292,7 @@
         tops.append(tile[0:2] + tile[2:4] + tile[4:6])
         totals.append(tile[6:8] + tile[8:10] + tile[10:12])
     top = functools.reduce(jnp.maximum, tops)
-    factors = [t * jnp.exp((m - top) * c) for m, t in zip(tops, totals)]
+    factors = [t * jnp.exp2(m - top) for m, t in zip(tops, totals)]
     whole = functools.reduce(jnp.add, factors)
     columns = jnp.transpose(jnp.concatenate([f / whole for f in factors], axis=0))
     for h in range(2):
@@ -303,11 +306,11 @@
             out_ref[z, at, :] = out
 
 
-def merge(got, c):
+def merge(got):
     parts, block, unused = got.shape
     block -= 16
     return pl.pallas_call(
-        functools.partial(merge_kernel, c=c),
+        merge_kernel,
         out_shape=jax.ShapeDtypeStruct((parts, block, HEAD), jnp.bfloat16),
         compiler_params=pltpu.CompilerParams(vmem_limit_bytes=16 * MiB),
         name="merge",
@@ -320,8 +323,7 @@
     items, pages_here, page_len, head = cache_keys.shape
     requests = counts.shape[0]
     kv_heads = items // requests
-    root = head**0.5
-    c = head**-0.5
+    c = head**-0.5 * LOG2E
     item = lax.axis_index("ctx")
     split_idx = lax.axis_index("split")
     first = (item * split_n + split_idx) * pages_here
@@ -338,11 +340,11 @@
     )
     marks = jnp.any(sel_row[None, None, :] == candidate[:, :, None], axis=2)
     live = jnp.sum(jnp.where(marks, mine, 0), axis=1)
-    cbias = jnp.where(marks, NEG, jnp.log(mine.astype(jnp.float32)) * root)
+    cbias = jnp.where(marks, NEG, jnp.log(mine.astype(jnp.float32)) * LOG2E)
     rows = queries.reshape(-1, head)
     partial = attend(live, cbias.reshape(1, -1), got, rows, split_n, c)
     shared = lax.all_to_all(partial, "split", split_axis=0, concat_axis=0, tiled=True)
-    out = lax.all_to_all(merge(shared, c), "split", split_axis=0, concat_axis=0, tiled=True)
+    out = lax.all_to_all(merge(shared), "split", split_axis=0, concat_axis=0, tiled=True)
     return out.astype(jnp.float32).reshape(queries.shape)
 
 

time: 132 us -> 131 us (level)
  the two profiles are of different devices: /device:TPU:7 before, /device:TPU:1 now
where the time goes in v4:
time: 131 us
  waiting for transfers between devices  51.3 us (39%)
  blocking collectives  49.7 us (38%)
  Pallas kernels  14.3 us (11%)
  starting transfers between devices  11.8 us (9%)
  local copies, waits for them, and re-layouts  2.17 us (2%)
  other arithmetic  1.4 us (1%)
    all_to_all x1, waiting for transfers between devices, local(): lax.all_to_all(message, 'ctx', split_axis=0, concat_axis=0, tiled=True)  51.3 us
    all_to_all x1, blocking collectives, local(): lax.all_to_all(partial, 'split', split_axis=0, concat_axis=0, tiled=True)  31.9 us
    all_to_all x1, blocking collectives, local(): lax.all_to_all(merge(shared), 'split', split_axis=0, concat_axis=0, tiled...  17.8 us
    all_to_all x1, starting transfers between devices, local(): lax.all_to_all(message, 'ctx', split_axis=0, concat_axis=0, tiled=True)  11.8 us
    pallas_call x1, Pallas kernels, attend(): pl.pallas_call(functools.partial(attend_kernel, chunk=chunk, block=block,...  9.29 us
    pallas_call x1, Pallas kernels, pack(): pl.pallas_call(pack_kernel, in_specs=[pl.BlockSpec(memory_space=pltpu.SME...  4.48 us
  transfers between devices with their start and end apart: 1, of which 1 were waited for; matrix products, arithmetic and copies ran while one was open for 2% of the time, Pallas kernels for 0%

profile of v4, /device:TPU:1, one launch (start us, length us, event | category | flops | bytes accessed | tf_op | source)
XLA Modules:
  0.0 130.7 jit_solution(11902104723087232259)
XLA Ops:
  0.0 4.5 %pack.1 = bf16[64,136,128]{2,1,0:T(8,128)(2,1)} custom-call(s32[1]{0:T(128)} %bitcast.2.page_ref, s32[16,1024]{1,0:T(8,128)} %counts_ref.1, s32[64,256]{1,0:T(8,128)} %listed_ref.1, bf16[64,2,64,128]{3,2,1,0:T(8,128)(2,1)} %keys_ref.1, bf16[64,2,64,128]{3,2,1,0:T(8,128)(2,1)} %values_ref.1), custom_call_target="tpu_custom_call" | custom-call | tf_op jit(solution)/shard_map/pack/pallas_call | solution.py:97
  4.5 0.0 copy-start
  4.5 11.8 %all-to-all-start = ((bf16[64,136,128]{2,1,0:T(8,128)(2,1)}), bf16[64,136,128]{2,1,0:T(8,128)(2,1)S(1)}, u32[]{:S(2)}, u32[]{:S(2)}) async-start(bf16[64,136,128]{2,1,0:T(8,128)(2,1)} %pack.1), calls=%async_computation | async-start | bytes 4456448 | tf_op jit(solution)/shard_map/all_to_all | solution.py:331
  16.3 0.7 constant_dynamic-slice_fusion.1
  17.0 0.2 compare_reduce_fusion
  17.2 0.1 copy.11
  17.3 0.2 reduce_or.12
  17.5 0.8 dynamic-slice_reduce_fusion
  18.3 0.2 reshape.78
  18.5 0.1 multiply_reduce_fusion
  18.6 0.1 mul.50
  18.8 0.1 copy.10
  18.9 51.3 %all-to-all-done.got_ref = bf16[64,136,128]{2,1,0:T(8,128)(2,1)S(1)} async-done(((bf16[64,136,128]{2,1,0:T(8,128)(2,1)}), bf16[64,136,128]{2,1,0:T(8,128)(2,1)S(1)}, u32[]{:S(2)}, u32[]{:S(2)}) %all-to-all-start) | async-done | bytes 2228256 | tf_op jit(solution)/shard_map/all_to_all | solution.py:331
  70.1 0.0 copy-done
  70.1 9.3 %attend.1 = bf16[8,272,128]{2,1,0:T(8,128)(2,1)S(1)} custom-call(s32[64]{0:T(128)S(1)} %fusion.live_ref, f32[1,128]{1,0:T(1,128)S(1)} %broadcast_select_fusion.cbias_ref, bf16[64,136,128]{2,1,0:T(8,128)(2,1)S(1)} %all-to-all-done.got_ref, bf16[2048,128]{1,0:T(8,128)(2,1)S(1)} %bitcast.9), custom_call_target="tpu_custom_call" | custom-call | flops 4429185024 | bytes 4194304 | tf_op jit(solution)/shard_map/attend/pallas_call | solution.py:255
  79.4 31.9 %all_to_all.15.got_ref = bf16[8,272,128]{2,1,0:T(8,128)(2,1)S(1)} all-to-all(bf16[8,272,128]{2,1,0:T(8,128)(2,1)S(1)} %attend.1), channel_id=1, replica_groups=mesh['ctx'=64,'split'=8] {'split'}, dimensions={0} | all-to-all | bytes 1114112 | tf_op jit(solution)/shard_map/all_to_all | solution.py:346
  111.3 0.5 merge.1
  111.8 17.8 %all_to_all.16 = bf16[8,256,128]{2,1,0:T(8,128)(2,1)S(1)} all-to-all(bf16[8,256,128]{2,1,0:T(8,128)(2,1)S(1)} %merge.1), channel_id=1, replica_groups=mesh['ctx'=64,'split'=8] {'split'}, dimensions={0} | all-to-all | bytes 1048576 | tf_op jit(solution)/shard_map/all_to_all | solution.py:347
  129.6 1.0 convert.1
  (4 shorter events, 0.0 us)
Async XLA Ops:
  4.5 65.6 %copy-start = (bf16[1,128,16,128]{3,2,1,0:T(8,128)(2,1)S(1)}, bf16[1,128,16,128]{3,2,1,0:T(8,128)(2,1)}, u32[]{:S(2)}) copy-start(bf16[1,128,16,128]{3,2,1,0:T(8,128)(2,1)} %param.9) | copy-start | bytes 1572868
  4.5 65.6 %all-to-all-start = ((bf16[64,136,128]{2,1,0:T(8,128)(2,1)}), bf16[64,136,128]{2,1,0:T(8,128)(2,1)S(1)}, u32[]{:S(2)}, u32[]{:S(2)}) async-start(bf16[64,136,128]{2,1,0:T(8,128)(2,1)} %pack.1), calls=%async_computation | async-start | bytes 4456448 | tf_op jit(solution)/shard_map/all_to_all | solution.py:331

commit v5 on v3

--- a/solution.py
+++ b/solution.py
@@ -14,6 +14,9 @@
 TAIL = 8
 ROWS = 2 * PAGE + TAIL
 MiB = 1024 * 1024
+
+RING = [3 * i % 8 for i in range(8)]
+CTX = [(x * 8 + y) * 2 + core for core in range(2) for x in range(4) for y in RING]
 
 
 def pack_kernel(
@@ -64,6 +67,7 @@
     quarter = slot // PAGE
     slot = slot % PAGE
     out_row = lax.broadcasted_iota(jnp.int32, (16, HEAD), 0)
+    ready = set()
     for g in range(groups):
         for copy in fetch(g):
             copy.wait()
@@ -78,13 +82,19 @@
                 inverse = 1.0 / divisor
             choice = jnp.broadcast_to(second[item : item + 1, :], (PAGE, HEAD)) > 0.5
             for a in range(2):
-                message[item, a * PAGE : (a + 1) * PAGE, :] = jnp.where(
+                message[CTX.index(item), a * PAGE : (a + 1) * PAGE, :] = jnp.where(
                     choice, cache[item, a, 1], cache[item, a, 0]
                 )
             both = cache[item].reshape(4 * PAGE, HEAD)
             total = jnp.dot(live, both, preferred_element_type=jnp.float32)
-            message[item, 2 * PAGE : ROWS, :] = (total * inverse)[:TAIL].astype(jnp.bfloat16)
-        send(g).start()
+            message[CTX.index(item), 2 * PAGE : ROWS, :] = (total * inverse)[:TAIL].astype(
+                jnp.bfloat16
+            )
+            ready.add(CTX.index(item))
+        for h in range(groups):
+            if ready.issuperset(range(h * block, (h + 1) * block)):
+                send(h).start()
+                ready.difference_update(range(h * block, (h + 1) * block))
     for g in range(groups):
         send(g).wait()
 
@@ -230,7 +240,7 @@
             pieces = split3(stats[0:1, :]) + split3(stats[1:2, :])
             row = lax.broadcasted_iota(jnp.int32, (16, HEAD), 0)
             for k in range(block // width):
-                to = (b - 1) * (block // width) + k
+                to = RING.index((b - 1) * (block // width) + k)
                 out_ref[to, :width, :] = out[k * width : (k + 1) * width, :]
                 tile = jnp.zeros((16, HEAD), jnp.float32)
                 for i, piece in enumerate(pieces):
@@ -314,6 +324,12 @@
     )(got)
 
 
+def exchange(blocks, axis, order):
+    return lax.all_to_all(
+        blocks, axis, split_axis=0, concat_axis=0, axis_index_groups=[order], tiled=True
+    )
+
+
 def local(cache_keys, cache_values, counts, listed, queries):
     ctx_n = lax.axis_size("ctx")
     split_n = lax.axis_size("split")
@@ -326,13 +342,15 @@
     split_idx = lax.axis_index("split")
     first = (item * split_n + split_idx) * pages_here
     message = pack(first.reshape(1), counts, listed, cache_keys, cache_values)
-    got = lax.all_to_all(message, "ctx", split_axis=0, concat_axis=0, tiled=True)
+    got = exchange(message, "ctx", CTX)
 
     sel_row = lax.dynamic_index_in_dim(listed, item, 0, keepdims=False)
     count_row = lax.dynamic_index_in_dim(counts, item // kv_heads, 0, keepdims=False)
     mine = count_row.reshape(ctx_n, split_n, pages_here)
     mine = lax.dynamic_index_in_dim(mine, split_idx, 1, keepdims=False)
-    source = jnp.arange(ctx_n, dtype=jnp.int32)[:, None]
+    mine = mine.reshape(4, 8, 2, pages_here).transpose(2, 0, 1, 3)
+    mine = jnp.stack([mine[:, :, y] for y in RING], axis=2).reshape(ctx_n, pages_here)
+    source = jnp.array(CTX, jnp.int32)[:, None]
     candidate = (source * split_n + split_idx) * pages_here + jnp.arange(
         pages_here, dtype=jnp.int32
     )
@@ -341,8 +359,9 @@
     cbias = jnp.where(marks, NEG, jnp.log(mine.astype(jnp.float32)) * root)
     rows = queries.reshape(-1, head)
     partial = attend(live, cbias.reshape(1, -1), got, rows, split_n, c)
-    shared = lax.all_to_all(partial, "split", split_axis=0, concat_axis=0, tiled=True)
-    out = lax.all_to_all(merge(shared, c), "split", split_axis=0, concat_axis=0, tiled=True)
+    shared = exchange(partial, "split", RING)
+    out = exchange(merge(shared, c), "split", RING)
+    out = jnp.concatenate([out[RING.index(z)] for z in range(split_n)], axis=0)
     return out.astype(jnp.float32).reshape(queries.shape)
 
 

time: 132 us -> 132 us (level)
  the two profiles are of different devices: /device:TPU:7 before, /device:TPU:10 now
where the time goes in v5:
time: 132 us
  blocking collectives  53.1 us (40%)
  waiting for transfers between devices  51.8 us (39%)
  Pallas kernels  12.1 us (9%)
  starting transfers between devices  10.7 us (8%)
  local copies, waits for them, and re-layouts  2.78 us (2%)
    all_to_all x2, blocking collectives, exchange(): lax.all_to_all(blocks, axis, split_axis=0, concat_axis=0, axis_index_grou...  53.1 us
    all_to_all x1, waiting for transfers between devices, exchange(): lax.all_to_all(blocks, axis, split_axis=0, concat_axis=0, axis_index_grou...  51.8 us
    all_to_all x1, starting transfers between devices, exchange(): lax.all_to_all(blocks, axis, split_axis=0, concat_axis=0, axis_index_grou...  10.7 us
    pallas_call x1, Pallas kernels, attend(): pl.pallas_call(functools.partial(attend_kernel, chunk=chunk, block=block,...  6.76 us
    pallas_call x1, Pallas kernels, pack(): pl.pallas_call(pack_kernel, in_specs=[pl.BlockSpec(memory_space=pltpu.SME...  4.85 us
  transfers between devices with their start and end apart: 1, of which 1 were waited for; matrix products, arithmetic and copies ran while one was open for 2% of the time, Pallas kernels for 0%

profile of v5, /device:TPU:10, one launch (start us, length us, event | category | flops | bytes accessed | tf_op | source)
XLA Modules:
  0.0 132.0 jit_solution(18221343610631829144)
XLA Ops:
  0.0 4.8 %pack.1 = bf16[64,136,128]{2,1,0:T(8,128)(2,1)} custom-call(s32[1]{0:T(128)} %bitcast.3.page_ref, s32[16,1024]{1,0:T(8,128)} %counts_ref.1, s32[64,256]{1,0:T(8,128)} %listed_ref.1, bf16[64,2,64,128]{3,2,1,0:T(8,128)(2,1)} %keys_ref.1, bf16[64,2,64,128]{3,2,1,0:T(8,128)(2,1)} %values_ref.1), custom_call_target="tpu_custom_call" | custom-call | tf_op jit(solution)/shard_map/pack/pallas_call | solution.py:106
  4.9 0.0 copy-start.1
  4.9 0.0 copy-start
  4.9 10.7 %all-to-all-start = ((bf16[64,136,128]{2,1,0:T(8,128)(2,1)}), bf16[64,136,128]{2,1,0:T(8,128)(2,1)S(1)}, u32[]{:S(2)}, u32[]{:S(2)}) async-start(bf16[64,136,128]{2,1,0:T(8,128)(2,1)} %pack.1), calls=%async_computation | async-start | bytes 4456448 | tf_op jit(solution)/shard_map/all_to_all | solution.py:328
  15.6 0.7 constant_dynamic-slice_fusion.1
  16.3 0.0 copy-done.1
  16.3 0.2 compare_reduce_fusion
  16.5 0.1 copy.33
  16.6 0.2 reduce_or.12
  16.8 0.8 dynamic-slice_reduce_fusion
  17.6 0.2 reshape.95
  17.8 0.1 copy.31
  17.9 0.1 fusion.8
  18.0 0.1 stack.5
  18.2 0.1 stack.6
  18.3 0.1 copy.34
  18.4 0.1 mul.42
  18.6 51.8 %all-to-all-done.got_ref = bf16[64,136,128]{2,1,0:T(8,128)(2,1)S(1)} async-done(((bf16[64,136,128]{2,1,0:T(8,128)(2,1)}), bf16[64,136,128]{2,1,0:T(8,128)(2,1)S(1)}, u32[]{:S(2)}, u32[]{:S(2)}) %all-to-all-start) | async-done | bytes 2228256 | tf_op jit(solution)/shard_map/all_to_all | solution.py:328
  70.4 0.0 copy-done
  70.4 6.8 %attend.1 = bf16[8,272,128]{2,1,0:T(8,128)(2,1)S(1)} custom-call(s32[64]{0:T(128)S(1)} %select_reduce_fusion.live_ref, f32[1,128]{1,0:T(1,128)S(1)} %broadcast_select_fusion.cbias_ref, bf16[64,136,128]{2,1,0:T(8,128)(2,1)S(1)} %all-to-all-done.got_ref, bf16[2048,128]{1,0:T(8,128)(2,1)S(1)} %bitcast.43), custom_call_target="tpu_custom_call" | custom-call | flops 4429185024 | bytes 4194304 | tf_op jit(solution)/shard_map/attend/pallas_call | solution.py:263
  77.2 32.0 %all_to_all.15.got_ref = bf16[8,272,128]{2,1,0:T(8,128)(2,1)S(1)} all-to-all(bf16[8,272,128]{2,1,0:T(8,128)(2,1)S(1)} %attend.1), channel_id=1, replica_groups={{0,3,6,1,4,7,2,5},{8,11,14,9,12,15,10,13},{16,19,22,17,20,23,18,21},{24..., dimensions={0} | all-to-all | bytes 1114112 | tf_op jit(solution)/shard_map/all_to_all | solution.py:328
  109.2 0.5 merge.1
  109.7 21.1 %all_to_all.16 = bf16[8,256,128]{2,1,0:T(8,128)(2,1)S(1)} all-to-all(bf16[8,256,128]{2,1,0:T(8,128)(2,1)S(1)} %merge.1), channel_id=1, replica_groups={{0,3,6,1,4,7,2,5},{8,11,14,9,12,15,10,13},{16,19,22,17,20,23,18,21},{24..., dimensions={0} | all-to-all | bytes 1048576 | tf_op jit(solution)/shard_map/all_to_all | solution.py:328
  131.0 1.0 convert.1
  (15 shorter events, 0.2 us)
Async XLA Ops:
  4.9 11.4 %copy-start.1 = (s32[64]{0:T(128)S(1)}, s32[64]{0:T(128)}, u32[]{:S(2)}) copy-start(s32[64]{0:T(128)} %constant.57) | copy-start | bytes 772
  4.9 65.5 %copy-start = (bf16[1,128,16,128]{3,2,1,0:T(8,128)(2,1)S(1)}, bf16[1,128,16,128]{3,2,1,0:T(8,128)(2,1)}, u32[]{:S(2)}) copy-start(bf16[1,128,16,128]{3,2,1,0:T(8,128)(2,1)} %param.10) | copy-start | bytes 1572868
  4.9 65.5 %all-to-all-start = ((bf16[64,136,128]{2,1,0:T(8,128)(2,1)}), bf16[64,136,128]{2,1,0:T(8,128)(2,1)S(1)}, u32[]{:S(2)}, u32[]{:S(2)}) async-start(bf16[64,136,128]{2,1,0:T(8,128)(2,1)} %pack.1), calls=%async_computation | async-start | bytes 4456448 | tf_op jit(solution)/shard_map/all_to_all | solution.py:328

commit v6 on v5

--- a/solution.py
+++ b/solution.py
@@ -141,23 +141,19 @@
     vv,
     ckt,
     cv,
-    cs0,
-    cs1,
-    sc0,
-    sc1,
+    cs,
+    sc,
     best,
     top,
     acc,
     *,
     chunk,
-    block,
     c,
 ):
     sources = got_ref.shape[0]
     cents = 2 * sources
     width = out_ref.shape[1] - 16
-    blocks = q_ref.shape[0] // block
-    sc, cs = (sc0, sc1), (cs0, cs1)
+    block = sc.shape[0]
 
     tails = got_ref[:, 2 * PAGE : ROWS, :].astype(jnp.float32).reshape(sources * TAIL, HEAD)
     tails = tails.astype(jnp.bfloat16)
@@ -200,68 +196,57 @@
 
     lax.fori_loop(0, chunks, turn, 0)
 
-    lanes = lax.broadcasted_iota(jnp.int32, (block, HEAD), 1)
-    for b in range(blocks + 1):
-        if b < blocks:
-            rows = q_ref[b * block : (b + 1) * block, :]
-            score = jnp.dot(rows, ckt[...], preferred_element_type=jnp.float32) + cbias_ref[...]
-            cs[b % 2][...] = score
-            best[...] = score
-        if b > 0:
-            weight = jnp.exp((cs[(b - 1) % 2][...] - top[...]) * c).astype(jnp.bfloat16)
-            acc[...] = jnp.dot(weight, cv[...], preferred_element_type=jnp.float32)
-
-        def body(j, carry, b=b):
+    for first in range(0, q_ref.shape[0], block):
+        score = jnp.dot(q_ref[first : first + block, :], ckt[...], preferred_element_type=jnp.float32) + cbias_ref[...]
+        cs[...] = score
+        best[...] = score
+
+        def scores(j, carry):
             at = pl.ds(pl.multiple_of(j * chunk, chunk), chunk)
-            if b > 0:
-                tops = jnp.concatenate([top[...]] * (chunk // HEAD), axis=1)
-                weight = jnp.exp((sc[(b - 1) % 2][:, at] - tops) * c).astype(jnp.bfloat16)
-                half = chunk // 2
-                for k in range(2):
-                    at_k = pl.ds(pl.multiple_of(j * chunk + k * half, half), half)
-                    acc[...] += jnp.dot(
-                        weight[:, k * half : (k + 1) * half],
-                        vv[at_k, :],
-                        preferred_element_type=jnp.float32,
-                    )
-            if b < blocks:
-                rows = q_ref[b * block : (b + 1) * block, :]
-                score = jnp.dot(rows, kt[:, at], preferred_element_type=jnp.float32)
-                sc[b % 2][:, at] = score
-                parts = [score[:, k : k + HEAD] for k in range(0, chunk, HEAD)]
-                best[...] = jnp.maximum(best[...], functools.reduce(jnp.maximum, parts))
+            score = jnp.dot(q_ref[first : first + block, :], kt[:, at], preferred_element_type=jnp.float32)
+            sc[:, at] = score
+            parts = [score[:, k : k + HEAD] for k in range(0, chunk, HEAD)]
+            best[...] = jnp.maximum(best[...], functools.reduce(jnp.maximum, parts))
             return carry
 
-        lax.fori_loop(0, chunks, body, 0)
-        if b > 0:
-            total = acc[:, HEAD:]
-            out = (acc[:, :HEAD] / total).astype(jnp.bfloat16)
-            stats = jnp.transpose(jnp.where(lanes == 0, top[...], total))
-            pieces = split3(stats[0:1, :]) + split3(stats[1:2, :])
-            row = lax.broadcasted_iota(jnp.int32, (16, HEAD), 0)
-            for k in range(block // width):
-                to = RING.index((b - 1) * (block // width) + k)
-                out_ref[to, :width, :] = out[k * width : (k + 1) * width, :]
-                tile = jnp.zeros((16, HEAD), jnp.float32)
-                for i, piece in enumerate(pieces):
-                    for h in range(2):
-                        from_ = k * width + h * HEAD
-                        tile = jnp.where(row == 2 * i + h, piece[:, from_ : from_ + HEAD], tile)
-                out_ref[to, width:, :] = tile.astype(jnp.bfloat16)
-        if b < blocks:
-            top[...] = jnp.broadcast_to(jnp.max(best[...], axis=1, keepdims=True), (block, HEAD))
+        lax.fori_loop(0, chunks, scores, 0)
+        top[...] = jnp.broadcast_to(jnp.max(best[...], axis=1, keepdims=True), (block, HEAD))
+        weight = jnp.exp((cs[...] - top[...]) * c).astype(jnp.bfloat16)
+        acc[...] = jnp.dot(weight, cv[...], preferred_element_type=jnp.float32)
+
+        def weighted(j, carry):
+            at = pl.ds(pl.multiple_of(j * chunk, chunk), chunk)
+            tops = jnp.concatenate([top[...]] * (chunk // HEAD), axis=1)
+            weight = jnp.exp((sc[:, at] - tops) * c).astype(jnp.bfloat16)
+            acc[...] += jnp.dot(weight, vv[at, :], preferred_element_type=jnp.float32)
+            return carry
+
+        lax.fori_loop(0, chunks, weighted, 0)
+        lanes = lax.broadcasted_iota(jnp.int32, (width, HEAD), 1)
+        row = lax.broadcasted_iota(jnp.int32, (16, HEAD), 0)
+        for z in range(block // width):
+            at = slice(z * width, (z + 1) * width)
+            to = RING.index(first // width + z)
+            total = acc[at, HEAD:]
+            out_ref[to, :width, :] = (acc[at, :HEAD] / total).astype(jnp.bfloat16)
+            stats = jnp.transpose(jnp.where(lanes == 0, top[at, :], total))
+            tile = jnp.zeros((16, HEAD), jnp.float32)
+            for i, piece in enumerate(split3(stats[0:1, :]) + split3(stats[1:2, :])):
+                for h in range(2):
+                    tile = jnp.where(row == 2 * i + h, piece[:, h * HEAD : (h + 1) * HEAD], tile)
+            out_ref[to, width:, :] = tile.astype(jnp.bfloat16)
 
 
 def attend(live, cbias, got, rows, parts, c):
     sources = got.shape[0]
     chunk = 512
-    block = 512
+    block = rows.shape[0] // 2
     slots = sources * PAGE
     cents = 2 * sources
     width = rows.shape[0] // parts
     vmem = pl.BlockSpec(memory_space=pltpu.VMEM)
     return pl.pallas_call(
-        functools.partial(attend_kernel, chunk=chunk, block=block, c=c),
+        functools.partial(attend_kernel, chunk=chunk, c=c),
         in_specs=[pl.BlockSpec(memory_space=pltpu.SMEM), vmem, vmem, vmem],
         out_specs=vmem,
         scratch_shapes=[
@@ -272,8 +257,6 @@
             pltpu.VMEM((HEAD, cents), jnp.bfloat16),
             pltpu.VMEM((cents, 2 * HEAD), jnp.bfloat16),
             pltpu.VMEM((block, cents), jnp.float32),
-            pltpu.VMEM((block, cents), jnp.float32),
-            pltpu.VMEM((block, slots), jnp.float32),
             pltpu.VMEM((block, slots), jnp.float32),
             pltpu.VMEM((block, HEAD), jnp.float32),
             pltpu.VMEM((block, HEAD), jnp.float32),

time: 132 us -> 130 us (0.985)
  the two profiles are of different devices: /device:TPU:10 before, /device:TPU:24 now
where the time goes in v6:
time: 130 us
  blocking collectives  51 us (39%)
  waiting for transfers between devices  50.3 us (39%)
  Pallas kernels  13.9 us (11%)
  starting transfers between devices  10.5 us (8%)
  local copies, waits for them, and re-layouts  2.78 us (2%)
    all_to_all x2, blocking collectives, exchange(): lax.all_to_all(blocks, axis, split_axis=0, concat_axis=0, axis_index_grou...  51 us
    all_to_all x1, waiting for transfers between devices, exchange(): lax.all_to_all(blocks, axis, split_axis=0, concat_axis=0, axis_index_grou...  50.3 us
    all_to_all x1, starting transfers between devices, exchange(): lax.all_to_all(blocks, axis, split_axis=0, concat_axis=0, axis_index_grou...  10.5 us
    pallas_call x1, Pallas kernels, attend(): pl.pallas_call(functools.partial(attend_kernel, chunk=chunk, c=c), in_spe...  8.55 us
    pallas_call x1, Pallas kernels, pack(): pl.pallas_call(pack_kernel, in_specs=[pl.BlockSpec(memory_space=pltpu.SME...  4.85 us
  transfers between devices with their start and end apart: 1, of which 1 were waited for; matrix products, arithmetic and copies ran while one was open for 2% of the time, Pallas kernels for 0%

profile of v6, /device:TPU:24, one launch (start us, length us, event | category | flops | bytes accessed | tf_op | source)
XLA Modules:
  0.0 129.9 jit_solution(18056636217382242164)
XLA Ops:
  0.0 4.8 %pack.1 = bf16[64,136,128]{2,1,0:T(8,128)(2,1)} custom-call(s32[1]{0:T(128)} %bitcast.3.page_ref, s32[16,1024]{1,0:T(8,128)} %counts_ref.1, s32[64,256]{1,0:T(8,128)} %listed_ref.1, bf16[64,2,64,128]{3,2,1,0:T(8,128)(2,1)} %keys_ref.1, bf16[64,2,64,128]{3,2,1,0:T(8,128)(2,1)} %values_ref.1), custom_call_target="tpu_custom_call" | custom-call | tf_op jit(solution)/shard_map/pack/pallas_call | solution.py:106
  4.9 0.0 copy-start.1
  4.9 0.0 copy-start
  4.9 10.5 %all-to-all-start = ((bf16[64,136,128]{2,1,0:T(8,128)(2,1)}), bf16[64,136,128]{2,1,0:T(8,128)(2,1)S(1)}, u32[]{:S(2)}, u32[]{:S(2)}) async-start(bf16[64,136,128]{2,1,0:T(8,128)(2,1)} %pack.1), calls=%async_computation | async-start | bytes 4456448 | tf_op jit(solution)/shard_map/all_to_all | solution.py:311
  15.4 0.7 constant_dynamic-slice_fusion.1
  16.1 0.0 copy-done.1
  16.1 0.2 compare_reduce_fusion
  16.3 0.1 copy.33
  16.4 0.2 reduce_or.12
  16.6 0.8 dynamic-slice_reduce_fusion
  17.4 0.2 reshape.95
  17.6 0.1 copy.31
  17.7 0.1 fusion.8
  17.8 0.1 stack.5
  18.0 0.1 stack.6
  18.1 0.1 copy.34
  18.2 0.1 mul.42
  18.4 50.3 %all-to-all-done.got_ref = bf16[64,136,128]{2,1,0:T(8,128)(2,1)S(1)} async-done(((bf16[64,136,128]{2,1,0:T(8,128)(2,1)}), bf16[64,136,128]{2,1,0:T(8,128)(2,1)S(1)}, u32[]{:S(2)}, u32[]{:S(2)}) %all-to-all-start) | async-done | bytes 2228256 | tf_op jit(solution)/shard_map/all_to_all | solution.py:311
  68.6 0.0 copy-done
  68.6 8.5 %attend.1 = bf16[8,272,128]{2,1,0:T(8,128)(2,1)S(1)} custom-call(s32[64]{0:T(128)S(1)} %select_reduce_fusion.live_ref, f32[1,128]{1,0:T(1,128)S(1)} %broadcast_select_fusion.cbias_ref, bf16[64,136,128]{2,1,0:T(8,128)(2,1)S(1)} %all-to-all-done.got_ref, bf16[2048,128]{1,0:T(8,128)(2,1)S(1)} %bitcast.43), custom_call_target="tpu_custom_call" | custom-call | flops 4429185024 | bytes 4194304 | tf_op jit(solution)/shard_map/attend/pallas_call | solution.py:248
  77.2 32.5 %all_to_all.15.got_ref = bf16[8,272,128]{2,1,0:T(8,128)(2,1)S(1)} all-to-all(bf16[8,272,128]{2,1,0:T(8,128)(2,1)S(1)} %attend.1), channel_id=1, replica_groups={{0,3,6,1,4,7,2,5},{8,11,14,9,12,15,10,13},{16,19,22,17,20,23,18,21},{24..., dimensions={0} | all-to-all | bytes 1114112 | tf_op jit(solution)/shard_map/all_to_all | solution.py:311
  109.7 0.5 merge.1
  110.2 18.5 %all_to_all.16 = bf16[8,256,128]{2,1,0:T(8,128)(2,1)S(1)} all-to-all(bf16[8,256,128]{2,1,0:T(8,128)(2,1)S(1)} %merge.1), channel_id=1, replica_groups={{0,3,6,1,4,7,2,5},{8,11,14,9,12,15,10,13},{16,19,22,17,20,23,18,21},{24..., dimensions={0} | all-to-all | bytes 1048576 | tf_op jit(solution)/shard_map/all_to_all | solution.py:311
  128.9 1.0 convert.1
  (15 shorter events, 0.2 us)
Async XLA Ops:
  4.9 11.2 %copy-start.1 = (s32[64]{0:T(128)S(1)}, s32[64]{0:T(128)}, u32[]{:S(2)}) copy-start(s32[64]{0:T(128)} %constant.57) | copy-start | bytes 772
  4.9 63.8 %copy-start = (bf16[1,128,16,128]{3,2,1,0:T(8,128)(2,1)S(1)}, bf16[1,128,16,128]{3,2,1,0:T(8,128)(2,1)}, u32[]{:S(2)}) copy-start(bf16[1,128,16,128]{3,2,1,0:T(8,128)(2,1)} %param.10) | copy-start | bytes 1572868
  4.9 63.8 %all-to-all-start = ((bf16[64,136,128]{2,1,0:T(8,128)(2,1)}), bf16[64,136,128]{2,1,0:T(8,128)(2,1)S(1)}, u32[]{:S(2)}, u32[]{:S(2)}) async-start(bf16[64,136,128]{2,1,0:T(8,128)(2,1)} %pack.1), calls=%async_computation | async-start | bytes 4456448 | tf_op jit(solution)/shard_map/all_to_all | solution.py:311

commit v7 on v6

--- a/solution.py
+++ b/solution.py
@@ -72,6 +72,13 @@
         for copy in fetch(g):
             copy.wait()
         for item in range(g * block, (g + 1) * block):
+            to = CTX.index(item)
+            choice = jnp.broadcast_to(second[item : item + 1, :], (PAGE, HEAD)) > 0.5
+            for a in range(2):
+                message[to, a * PAGE : (a + 1) * PAGE, :] = jnp.where(
+                    choice, cache[item, a, 1], cache[item, a, 0]
+                )
+        for item in range(g * block, (g + 1) * block, 2):
             if item % kv_heads == 0:
                 request = item // kv_heads
                 count = [count_here[request, page % HEAD + p] for p in range(2)]
@@ -80,17 +87,14 @@
                 live = jnp.where(live, 1.0, 0.0).astype(jnp.bfloat16)
                 divisor = jnp.where(out_row % 2 == 0, count[0], count[1]).astype(jnp.float32)
                 inverse = 1.0 / divisor
-            choice = jnp.broadcast_to(second[item : item + 1, :], (PAGE, HEAD)) > 0.5
-            for a in range(2):
-                message[CTX.index(item), a * PAGE : (a + 1) * PAGE, :] = jnp.where(
-                    choice, cache[item, a, 1], cache[item, a, 0]
-                )
-            both = cache[item].reshape(4 * PAGE, HEAD)
+            both = jnp.concatenate(
+                [cache[i].reshape(4 * PAGE, HEAD) for i in (item, item + 1)], axis=1
+            )
             total = jnp.dot(live, both, preferred_element_type=jnp.float32)
-            message[CTX.index(item), 2 * PAGE : ROWS, :] = (total * inverse)[:TAIL].astype(
-                jnp.bfloat16
-            )
-            ready.add(CTX.index(item))
+            for k in range(2):
+                mean = total[:, k * HEAD : (k + 1) * HEAD] * inverse
+                message[CTX.index(item + k), 2 * PAGE : ROWS, :] = mean[:TAIL].astype(jnp.bfloat16)
+        ready.update(CTX.index(item) for item in range(g * block, (g + 1) * block))
         for h in range(groups):
             if ready.issuperset(range(h * block, (h + 1) * block)):
                 send(h).start()
@@ -179,7 +183,9 @@
         return at + live_ref[s]
 
     end = lax.fori_loop(0, sources, place, 0, unroll=4)
-    chunks = (end + chunk - 1) // chunk
+    half = chunk // 2
+    halves = (end + half - 1) // half
+    chunks = halves // 2
     rest = pl.ds(end, chunk)
     keys[rest, :] = jnp.broadcast_to(keys[0:1, :], (chunk, HEAD))
     values[rest, :] = jnp.zeros((chunk, HEAD), jnp.float32)
@@ -194,34 +200,43 @@
             vv[at, HEAD:] = jnp.where(number + start < end, 1.0, 0.0).astype(jnp.bfloat16)
         return carry
 
-    lax.fori_loop(0, chunks, turn, 0)
+    lax.fori_loop(0, (halves + 1) // 2, turn, 0)
+
+    def each_chunk(body):
+        def whole(j, carry):
+            body(pl.ds(pl.multiple_of(j * chunk, chunk), chunk))
+            return carry
+
+        lax.fori_loop(0, chunks, whole, 0)
+
+        @pl.when(halves % 2 == 1)
+        def _():
+            body(pl.ds(pl.multiple_of(chunks * chunk, chunk), half))
 
     for first in range(0, q_ref.shape[0], block):
         score = jnp.dot(q_ref[first : first + block, :], ckt[...], preferred_element_type=jnp.float32) + cbias_ref[...]
         cs[...] = score
         best[...] = score
 
-        def scores(j, carry):
-            at = pl.ds(pl.multiple_of(j * chunk, chunk), chunk)
-            score = jnp.dot(q_ref[first : first + block, :], kt[:, at], preferred_element_type=jnp.float32)
+        def scores(at, first=first):
+            score = jnp.dot(
+                q_ref[first : first + block, :], kt[:, at], preferred_element_type=jnp.float32
+            )
             sc[:, at] = score
-            parts = [score[:, k : k + HEAD] for k in range(0, chunk, HEAD)]
+            parts = [score[:, k : k + HEAD] for k in range(0, at.size, HEAD)]
             best[...] = jnp.maximum(best[...], functools.reduce(jnp.maximum, parts))
-            return carry
-
-        lax.fori_loop(0, chunks, scores, 0)
+
+        each_chunk(scores)
         top[...] = jnp.broadcast_to(jnp.max(best[...], axis=1, keepdims=True), (block, HEAD))
         weight = jnp.exp((cs[...] - top[...]) * c).astype(jnp.bfloat16)
         acc[...] = jnp.dot(weight, cv[...], preferred_element_type=jnp.float32)
 
-        def weighted(j, carry):
-            at = pl.ds(pl.multiple_of(j * chunk, chunk), chunk)
-            tops = jnp.concatenate([top[...]] * (chunk // HEAD), axis=1)
+        def weighted(at):
+            tops = jnp.concatenate([top[...]] * (at.size // HEAD), axis=1)
             weight = jnp.exp((sc[:, at] - tops) * c).astype(jnp.bfloat16)
             acc[...] += jnp.dot(weight, vv[at, :], preferred_element_type=jnp.float32)
-            return carry
-
-        lax.fori_loop(0, chunks, weighted, 0)
+
+        each_chunk(weighted)
         lanes = lax.broadcasted_iota(jnp.int32, (width, HEAD), 1)
         row = lax.broadcasted_iota(jnp.int32, (16, HEAD), 0)
         for z in range(block // width):

time: 130 us -> 130 us (level)
  Pallas kernels: 13.9 us -> 11.2 us
  blocking collectives: 51 us -> 53 us
    pallas_call x1, Pallas kernels: 8.55 us -> 5.87 us  [attend(): pl.pallas_call(functools.partial(attend_kernel, chunk=chunk, c=c), in_spe...]
    all_to_all x2, blocking collectives: 51 us -> 53 us  [exchange(): lax.all_to_all(blocks, axis, split_axis=0, concat_axis=0, axis_index_grou...]
where the time goes in v7:
time: 130 us; the launch traced here: 129 us
  blocking collectives  53 us (41%)
  waiting for transfers between devices  50.3 us (39%)
  Pallas kernels  11.2 us (9%)
  starting transfers between devices  10.5 us (8%)
  local copies, waits for them, and re-layouts  2.78 us (2%)
    all_to_all x2, blocking collectives, exchange(): lax.all_to_all(blocks, axis, split_axis=0, concat_axis=0, axis_index_grou...  53 us
    all_to_all x1, waiting for transfers between devices, exchange(): lax.all_to_all(blocks, axis, split_axis=0, concat_axis=0, axis_index_grou...  50.3 us
    all_to_all x1, starting transfers between devices, exchange(): lax.all_to_all(blocks, axis, split_axis=0, concat_axis=0, axis_index_grou...  10.5 us
    pallas_call x1, Pallas kernels, attend(): pl.pallas_call(functools.partial(attend_kernel, chunk=chunk, c=c), in_spe...  5.87 us
    pallas_call x1, Pallas kernels, pack(): pl.pallas_call(pack_kernel, in_specs=[pl.BlockSpec(memory_space=pltpu.SME...  4.84 us
  transfers between devices with their start and end apart: 1, of which 1 were waited for; matrix products, arithmetic and copies ran while one was open for 2% of the time, Pallas kernels for 0%

profile of v7, /device:TPU:24, one launch (start us, length us, event | category | flops | bytes accessed | tf_op | source)
XLA Modules:
  0.0 129.2 jit_solution(17162983471630220234)
XLA Ops:
  0.0 4.8 %pack.1 = bf16[64,136,128]{2,1,0:T(8,128)(2,1)} custom-call(s32[1]{0:T(128)} %bitcast.3.page_ref, s32[16,1024]{1,0:T(8,128)} %counts_ref.1, s32[64,256]{1,0:T(8,128)} %listed_ref.1, bf16[64,2,64,128]{3,2,1,0:T(8,128)(2,1)} %keys_ref.1, bf16[64,2,64,128]{3,2,1,0:T(8,128)(2,1)} %values_ref.1), custom_call_target="tpu_custom_call" | custom-call | tf_op jit(solution)/shard_map/pack/pallas_call | solution.py:110
  4.9 0.0 copy-start.1
  4.9 0.0 copy-start
  4.9 10.5 %all-to-all-start = ((bf16[64,136,128]{2,1,0:T(8,128)(2,1)}), bf16[64,136,128]{2,1,0:T(8,128)(2,1)S(1)}, u32[]{:S(2)}, u32[]{:S(2)}) async-start(bf16[64,136,128]{2,1,0:T(8,128)(2,1)} %pack.1), calls=%async_computation | async-start | bytes 4456448 | tf_op jit(solution)/shard_map/all_to_all | solution.py:326
  15.4 0.7 constant_dynamic-slice_fusion.1
  16.1 0.0 copy-done.1
  16.1 0.2 compare_reduce_fusion
  16.3 0.1 copy.33
  16.4 0.2 reduce_or.12
  16.6 0.8 dynamic-slice_reduce_fusion
  17.4 0.2 reshape.95
  17.6 0.1 copy.31
  17.7 0.1 fusion.8
  17.8 0.1 stack.5
  18.0 0.1 stack.6
  18.1 0.1 copy.34
  18.2 0.1 mul.42
  18.4 50.3 %all-to-all-done.got_ref = bf16[64,136,128]{2,1,0:T(8,128)(2,1)S(1)} async-done(((bf16[64,136,128]{2,1,0:T(8,128)(2,1)}), bf16[64,136,128]{2,1,0:T(8,128)(2,1)S(1)}, u32[]{:S(2)}, u32[]{:S(2)}) %all-to-all-start) | async-done | bytes 2228256 | tf_op jit(solution)/shard_map/all_to_all | solution.py:326
  68.6 0.0 copy-done
  68.6 5.9 %attend.1 = bf16[8,272,128]{2,1,0:T(8,128)(2,1)S(1)} custom-call(s32[64]{0:T(128)S(1)} %select_reduce_fusion.live_ref, f32[1,128]{1,0:T(1,128)S(1)} %broadcast_select_fusion.cbias_ref, bf16[64,136,128]{2,1,0:T(8,128)(2,1)S(1)} %all-to-all-done.got_ref, bf16[2048,128]{1,0:T(8,128)(2,1)S(1)} %bitcast.43), custom_call_target="tpu_custom_call" | custom-call | flops 4429185024 | bytes 4194304 | tf_op jit(solution)/shard_map/attend/pallas_call | solution.py:263
  74.5 34.5 %all_to_all.15.got_ref = bf16[8,272,128]{2,1,0:T(8,128)(2,1)S(1)} all-to-all(bf16[8,272,128]{2,1,0:T(8,128)(2,1)S(1)} %attend.1), channel_id=1, replica_groups={{0,3,6,1,4,7,2,5},{8,11,14,9,12,15,10,13},{16,19,22,17,20,23,18,21},{24..., dimensions={0} | all-to-all | bytes 1114112 | tf_op jit(solution)/shard_map/all_to_all | solution.py:326
  109.0 0.5 merge.1
  109.6 18.5 %all_to_all.16 = bf16[8,256,128]{2,1,0:T(8,128)(2,1)S(1)} all-to-all(bf16[8,256,128]{2,1,0:T(8,128)(2,1)S(1)} %merge.1), channel_id=1, replica_groups={{0,3,6,1,4,7,2,5},{8,11,14,9,12,15,10,13},{16,19,22,17,20,23,18,21},{24..., dimensions={0} | all-to-all | bytes 1048576 | tf_op jit(solution)/shard_map/all_to_all | solution.py:326
  128.2 1.0 convert.1
  (15 shorter events, 0.2 us)
Async XLA Ops:
  4.9 11.2 %copy-start.1 = (s32[64]{0:T(128)S(1)}, s32[64]{0:T(128)}, u32[]{:S(2)}) copy-start(s32[64]{0:T(128)} %constant.57) | copy-start | bytes 772
  4.9 63.8 %copy-start = (bf16[1,128,16,128]{3,2,1,0:T(8,128)(2,1)S(1)}, bf16[1,128,16,128]{3,2,1,0:T(8,128)(2,1)}, u32[]{:S(2)}) copy-start(bf16[1,128,16,128]{3,2,1,0:T(8,128)(2,1)} %param.10) | copy-start | bytes 1572868
  4.9 63.8 %all-to-all-start = ((bf16[64,136,128]{2,1,0:T(8,128)(2,1)}), bf16[64,136,128]{2,1,0:T(8,128)(2,1)S(1)}, u32[]{:S(2)}, u32[]{:S(2)}) async-start(bf16[64,136,128]{2,1,0:T(8,128)(2,1)} %pack.1), calls=%async_computation | async-start | bytes 4456448 | tf_op jit(solution)/shard_map/all_to_all | solution.py:326

commit v8 on v7

--- a/solution.py
+++ b/solution.py
@@ -37,7 +37,7 @@
     items = out_ref.shape[0]
     page = page_ref[0]
     kv_heads = 4
-    block = 8
+    block = 4
     groups = items // block
 
     def fetch(g):
@@ -47,9 +47,9 @@
             for a, ref in enumerate((keys_ref, values_ref))
         ]
 
-    def send(g):
-        at = pl.ds(g * block, block)
-        return pltpu.make_async_copy(message.at[at], out_ref.at[at], sent.at[g])
+    def send(item):
+        to = CTX.index(item)
+        return pltpu.make_async_copy(message.at[to], out_ref.at[to], sent.at[item])
 
     columns = pl.ds(pl.multiple_of((page // HEAD) * HEAD, HEAD), HEAD)
     lists = pltpu.make_async_copy(listed_ref, listed, small.at[0])
@@ -57,8 +57,8 @@
     lists.start()
     numbers.start()
     for g in range(groups):
-        for copy in fetch(g):
-            copy.start()
+        for a, copy in enumerate(fetch(g)):
+            copy.start(priority=a)
     lists.wait()
     second = jnp.max(jnp.where(listed[...] == page + 1, 1.0, 0.0), axis=1, keepdims=True)
     numbers.wait()
@@ -67,7 +67,6 @@
     quarter = slot // PAGE
     slot = slot % PAGE
     out_row = lax.broadcasted_iota(jnp.int32, (16, HEAD), 0)
-    ready = set()
     for g in range(groups):
         for copy in fetch(g):
             copy.wait()
@@ -94,18 +93,15 @@
             for k in range(2):
                 mean = total[:, k * HEAD : (k + 1) * HEAD] * inverse
                 message[CTX.index(item + k), 2 * PAGE : ROWS, :] = mean[:TAIL].astype(jnp.bfloat16)
-        ready.update(CTX.index(item) for item in range(g * block, (g + 1) * block))
-        for h in range(groups):
-            if ready.issuperset(range(h * block, (h + 1) * block)):
-                send(h).start()
-                ready.difference_update(range(h * block, (h + 1) * block))
-    for g in range(groups):
-        send(g).wait()
+            for i in (item, item + 1):
+                send(i).start(priority=i % 2)
+    for item in range(items):
+        send(item).wait()
 
 
 def pack(page, counts, listed, cache_keys, cache_values):
     items = cache_keys.shape[0]
-    groups = items // 8
+    groups = items // 4
     whole = pl.BlockSpec(memory_space=pl.ANY)
     return pl.pallas_call(
         pack_kernel,
@@ -118,7 +114,7 @@
             pltpu.SMEM((counts.shape[0], HEAD), jnp.int32),
             pltpu.VMEM(listed.shape, jnp.int32),
             pltpu.SemaphoreType.DMA((2, groups)),
-            pltpu.SemaphoreType.DMA((groups,)),
+            pltpu.SemaphoreType.DMA((items,)),
             pltpu.SemaphoreType.DMA((2,)),
         ],
         compiler_params=pltpu.CompilerParams(vmem_limit_bytes=58 * MiB),
@@ -141,7 +137,7 @@
     out_ref,
     keys,
     values,
-    kt,
+    kb,
     vv,
     ckt,
     cv,
@@ -156,7 +152,7 @@
 ):
     sources = got_ref.shape[0]
     cents = 2 * sources
-    width = out_ref.shape[1] - 16
+    width = out_ref.shape[1] - TAIL
     block = sc.shape[0]
 
     tails = got_ref[:, 2 * PAGE : ROWS, :].astype(jnp.float32).reshape(sources * TAIL, HEAD)
@@ -195,7 +191,7 @@
         for k in range(0, chunk, HEAD):
             start = pl.multiple_of(j * chunk + k, HEAD)
             at = pl.ds(start, HEAD)
-            kt[:, at] = jnp.transpose(keys[at, :]).astype(jnp.bfloat16)
+            kb[at, :] = keys[at, :].astype(jnp.bfloat16)
             vv[at, :HEAD] = values[at, :].astype(jnp.bfloat16)
             vv[at, HEAD:] = jnp.where(number + start < end, 1.0, 0.0).astype(jnp.bfloat16)
         return carry
@@ -219,8 +215,11 @@
         best[...] = score
 
         def scores(at, first=first):
-            score = jnp.dot(
-                q_ref[first : first + block, :], kt[:, at], preferred_element_type=jnp.float32
+            score = lax.dot_general(
+                q_ref[first : first + block, :],
+                kb[at, :],
+                (((1,), (1,)), ((), ())),
+                preferred_element_type=jnp.float32,
             )
             sc[:, at] = score
             parts = [score[:, k : k + HEAD] for k in range(0, at.size, HEAD)]
@@ -237,16 +236,15 @@
             acc[...] += jnp.dot(weight, vv[at, :], preferred_element_type=jnp.float32)
 
         each_chunk(weighted)
-        lanes = lax.broadcasted_iota(jnp.int32, (width, HEAD), 1)
-        row = lax.broadcasted_iota(jnp.int32, (16, HEAD), 0)
+        row = lax.broadcasted_iota(jnp.int32, (TAIL, HEAD), 0)
         for z in range(block // width):
             at = slice(z * width, (z + 1) * width)
             to = RING.index(first // width + z)
             total = acc[at, HEAD:]
             out_ref[to, :width, :] = (acc[at, :HEAD] / total).astype(jnp.bfloat16)
-            stats = jnp.transpose(jnp.where(lanes == 0, top[at, :], total))
-            tile = jnp.zeros((16, HEAD), jnp.float32)
-            for i, piece in enumerate(split3(stats[0:1, :]) + split3(stats[1:2, :])):
+            stats = jnp.transpose(top[at, :] + jnp.log(total) * (1.0 / c))
+            tile = jnp.zeros((TAIL, HEAD), jnp.float32)
+            for i, piece in enumerate(split3(stats[0:1, :])):
                 for h in range(2):
                     tile = jnp.where(row == 2 * i + h, piece[:, h * HEAD : (h + 1) * HEAD], tile)
             out_ref[to, width:, :] = tile.astype(jnp.bfloat16)
@@ -267,7 +265,7 @@
         scratch_shapes=[
             pltpu.VMEM((slots + chunk, HEAD), jnp.float32),
             pltpu.VMEM((slots + chunk, HEAD), jnp.float32),
-            pltpu.VMEM((HEAD, slots), jnp.bfloat16),
+            pltpu.VMEM((slots, HEAD), jnp.bfloat16),
             pltpu.VMEM((slots, 2 * HEAD), jnp.bfloat16),
             pltpu.VMEM((HEAD, cents), jnp.bfloat16),
             pltpu.VMEM((cents, 2 * HEAD), jnp.bfloat16),
@@ -277,7 +275,7 @@
             pltpu.VMEM((block, HEAD), jnp.float32),
             pltpu.VMEM((block, 2 * HEAD), jnp.float32),
         ],
-        out_shape=jax.ShapeDtypeStruct((parts, width + 16, HEAD), jnp.bfloat16),
+        out_shape=jax.ShapeDtypeStruct((parts, width + TAIL, HEAD), jnp.bfloat16),
         compiler_params=pltpu.CompilerParams(vmem_limit_bytes=40 * MiB),
         cost_estimate=pl.CostEstimate(
             flops=4 * rows.shape[0] * (slots + cents) * HEAD,
@@ -291,13 +289,12 @@
 def merge_kernel(got_ref, out_ref, *, c):
     parts = got_ref.shape[0]
     block = out_ref.shape[1]
-    tops, totals = [], []
+    sums = []
     for z in range(parts):
         tile = got_ref[z, block:, :].astype(jnp.float32)
-        tops.append(tile[0:2] + tile[2:4] + tile[4:6])
-        totals.append(tile[6:8] + tile[8:10] + tile[10:12])
-    top = functools.reduce(jnp.maximum, tops)
-    factors = [t * jnp.exp((m - top) * c) for m, t in zip(tops, totals)]
+        sums.append(tile[0:2] + tile[2:4] + tile[4:6])
+    top = functools.reduce(jnp.maximum, sums)
+    factors = [jnp.exp((m - top) * c) for m in sums]
     whole = functools.reduce(jnp.add, factors)
     columns = jnp.transpose(jnp.concatenate([f / whole for f in factors], axis=0))
     for h in range(2):
@@ -313,7 +310,7 @@
 
 def merge(got, c):
     parts, block, unused = got.shape
-    block -= 16
+    block -= TAIL
     return pl.pallas_call(
         functools.partial(merge_kernel, c=c),
         out_shape=jax.ShapeDtypeStruct((parts, block, HEAD), jnp.bfloat16),

time: 130 us -> 128 us (0.985)
  the two profiles are of different devices: /device:TPU:24 before, /device:TPU:1 now
where the time goes in v8:
time: 128 us; the launch traced here: 126 us
  waiting for transfers between devices  49 us (38%)
  blocking collectives  47.3 us (37%)
  Pallas kernels  14.1 us (11%)
  starting transfers between devices  11.9 us (9%)
  local copies, waits for them, and re-layouts  2.78 us (2%)
  other arithmetic  1.28 us (1%)
    all_to_all x1, waiting for transfers between devices, exchange(): lax.all_to_all(blocks, axis, split_axis=0, concat_axis=0, axis_index_grou...  49 us
    all_to_all x2, blocking collectives, exchange(): lax.all_to_all(blocks, axis, split_axis=0, concat_axis=0, axis_index_grou...  47.3 us
    all_to_all x1, starting transfers between devices, exchange(): lax.all_to_all(blocks, axis, split_axis=0, concat_axis=0, axis_index_grou...  11.9 us
    pallas_call x1, Pallas kernels, attend(): pl.pallas_call(functools.partial(attend_kernel, chunk=chunk, c=c), in_spe...  7.86 us
    pallas_call x1, Pallas kernels, pack(): pl.pallas_call(pack_kernel, in_specs=[pl.BlockSpec(memory_space=pltpu.SME...  5.69 us
  transfers between devices with their start and end apart: 1, of which 1 were waited for; matrix products, arithmetic and copies ran while one was open for 2% of the time, Pallas kernels for 0%

profile of v8, /device:TPU:1, one launch (start us, length us, event | category | flops | bytes accessed | tf_op | source)
XLA Modules:
  0.0 126.4 jit_solution(739597913234687087)
XLA Ops:
  0.0 5.7 %pack.1 = bf16[64,136,128]{2,1,0:T(8,128)(2,1)} custom-call(s32[1]{0:T(128)} %bitcast.3.page_ref, s32[16,1024]{1,0:T(8,128)} %counts_ref.1, s32[64,256]{1,0:T(8,128)} %listed_ref.1, bf16[64,2,64,128]{3,2,1,0:T(8,128)(2,1)} %keys_ref.1, bf16[64,2,64,128]{3,2,1,0:T(8,128)(2,1)} %values_ref.1), custom_call_target="tpu_custom_call" | custom-call | tf_op jit(solution)/shard_map/pack/pallas_call | solution.py:106
  5.7 0.0 copy-start.1
  5.7 0.0 copy-start
  5.7 11.9 %all-to-all-start = ((bf16[64,136,128]{2,1,0:T(8,128)(2,1)}), bf16[64,136,128]{2,1,0:T(8,128)(2,1)S(1)}, u32[]{:S(2)}, u32[]{:S(2)}) async-start(bf16[64,136,128]{2,1,0:T(8,128)(2,1)} %pack.1), calls=%async_computation | async-start | bytes 4456448 | tf_op jit(solution)/shard_map/all_to_all | solution.py:323
  17.6 0.7 constant_dynamic-slice_fusion.1
  18.3 0.0 copy-done.1
  18.3 0.2 compare_reduce_fusion
  18.5 0.1 copy.33
  18.6 0.2 reduce_or.12
  18.8 0.8 dynamic-slice_reduce_fusion
  19.6 0.2 reshape.95
  19.8 0.1 copy.31
  19.9 0.1 fusion.8
  20.0 0.1 stack.5
  20.2 0.1 stack.6
  20.3 0.1 copy.34
  20.4 0.1 mul.42
  20.6 49.0 %all-to-all-done.got_ref = bf16[64,136,128]{2,1,0:T(8,128)(2,1)S(1)} async-done(((bf16[64,136,128]{2,1,0:T(8,128)(2,1)}), bf16[64,136,128]{2,1,0:T(8,128)(2,1)S(1)}, u32[]{:S(2)}, u32[]{:S(2)}) %all-to-all-start) | async-done | bytes 2228256 | tf_op jit(solution)/shard_map/all_to_all | solution.py:323
  69.6 0.0 copy-done
  69.6 7.9 %attend.1 = bf16[8,264,128]{2,1,0:T(8,128)(2,1)S(1)} custom-call(s32[64]{0:T(128)S(1)} %select_reduce_fusion.live_ref, f32[1,128]{1,0:T(1,128)S(1)} %broadcast_select_fusion.cbias_ref, bf16[64,136,128]{2,1,0:T(8,128)(2,1)S(1)} %all-to-all-done.got_ref, bf16[2048,128]{1,0:T(8,128)(2,1)S(1)} %bitcast.43), custom_call_target="tpu_custom_call" | custom-call | flops 4429185024 | bytes 4194304 | tf_op jit(solution)/shard_map/attend/pallas_call | solution.py:261
  77.4 29.0 %all_to_all.15.got_ref = bf16[8,264,128]{2,1,0:T(8,128)(2,1)S(1)} all-to-all(bf16[8,264,128]{2,1,0:T(8,128)(2,1)S(1)} %attend.1), channel_id=1, replica_groups={{0,3,6,1,4,7,2,5},{8,11,14,9,12,15,10,13},{16,19,22,17,20,23,18,21},{24..., dimensions={0} | all-to-all | bytes 1081344 | tf_op jit(solution)/shard_map/all_to_all | solution.py:323
  106.5 0.5 merge.1
  107.0 18.3 %all_to_all.16 = bf16[8,256,128]{2,1,0:T(8,128)(2,1)S(1)} all-to-all(bf16[8,256,128]{2,1,0:T(8,128)(2,1)S(1)} %merge.1), channel_id=1, replica_groups={{0,3,6,1,4,7,2,5},{8,11,14,9,12,15,10,13},{16,19,22,17,20,23,18,21},{24..., dimensions={0} | all-to-all | bytes 1048576 | tf_op jit(solution)/shard_map/all_to_all | solution.py:323
  125.4 1.0 convert.1
  (15 shorter events, 0.2 us)
Async XLA Ops:
  5.7 12.6 %copy-start.1 = (s32[64]{0:T(128)S(1)}, s32[64]{0:T(128)}, u32[]{:S(2)}) copy-start(s32[64]{0:T(128)} %constant.57) | copy-start | bytes 772
  5.7 63.8 %copy-start = (bf16[1,128,16,128]{3,2,1,0:T(8,128)(2,1)S(1)}, bf16[1,128,16,128]{3,2,1,0:T(8,128)(2,1)}, u32[]{:S(2)}) copy-start(bf16[1,128,16,128]{3,2,1,0:T(8,128)(2,1)} %param.10) | copy-start | bytes 1572868
  5.7 63.8 %all-to-all-start = ((bf16[64,136,128]{2,1,0:T(8,128)(2,1)}), bf16[64,136,128]{2,1,0:T(8,128)(2,1)S(1)}, u32[]{:S(2)}, u32[]{:S(2)}) async-start(bf16[64,136,128]{2,1,0:T(8,128)(2,1)} %pack.1), calls=%async_computation | async-start | bytes 4456448 | tf_op jit(solution)/shard_map/all_to_all | solution.py:323

commit v9 on v8

--- a/solution.py
+++ b/solution.py
@@ -17,6 +17,11 @@
 
 RING = [3 * i % 8 for i in range(8)]
 CTX = [(x * 8 + y) * 2 + core for core in range(2) for x in range(4) for y in RING]
+
+
+GROUPS = [(0, 24), (24, 24), (48, 16)]
+SENDS = [(at, 8) for at in range(0, 64, 8) if CTX[at] < 48]
+SENDS += [(at, 1) for at in range(64) if CTX[at] >= 48]
 
 
 def pack_kernel(
@@ -37,26 +42,24 @@
     items = out_ref.shape[0]
     page = page_ref[0]
     kv_heads = 4
-    block = 4
-    groups = items // block
 
     def fetch(g):
-        at = pl.ds(g * block, block)
+        at = pl.ds(GROUPS[g][0], GROUPS[g][1])
         return [
-            pltpu.make_async_copy(ref.at[at], cache.at[at, a], got.at[a, g])
+            pltpu.make_async_copy(ref.at[at], cache.at[a, at], got.at[a, g])
             for a, ref in enumerate((keys_ref, values_ref))
         ]
 
-    def send(item):
-        to = CTX.index(item)
-        return pltpu.make_async_copy(message.at[to], out_ref.at[to], sent.at[item])
+    def send(k):
+        at = pl.ds(SENDS[k][0], SENDS[k][1])
+        return pltpu.make_async_copy(message.at[at], out_ref.at[at], sent.at[k])
 
     columns = pl.ds(pl.multiple_of((page // HEAD) * HEAD, HEAD), HEAD)
     lists = pltpu.make_async_copy(listed_ref, listed, small.at[0])
     numbers = pltpu.make_async_copy(counts_ref.at[:, columns], count_here, small.at[1])
     lists.start()
     numbers.start()
-    for g in range(groups):
+    for g in range(len(GROUPS)):
         for a, copy in enumerate(fetch(g)):
             copy.start(priority=a)
     lists.wait()
@@ -67,17 +70,18 @@
     quarter = slot // PAGE
     slot = slot % PAGE
     out_row = lax.broadcasted_iota(jnp.int32, (16, HEAD), 0)
-    for g in range(groups):
+    ready = set()
+    for g, (first, number) in enumerate(GROUPS):
         for copy in fetch(g):
             copy.wait()
-        for item in range(g * block, (g + 1) * block):
+        for item in range(first, first + number):
             to = CTX.index(item)
             choice = jnp.broadcast_to(second[item : item + 1, :], (PAGE, HEAD)) > 0.5
             for a in range(2):
                 message[to, a * PAGE : (a + 1) * PAGE, :] = jnp.where(
-                    choice, cache[item, a, 1], cache[item, a, 0]
+                    choice, cache[a, item, 1], cache[a, item, 0]
                 )
-        for item in range(g * block, (g + 1) * block, 2):
+        for item in range(first, first + number, 2):
             if item % kv_heads == 0:
                 request = item // kv_heads
                 count = [count_here[request, page % HEAD + p] for p in range(2)]
@@ -87,21 +91,27 @@
                 divisor = jnp.where(out_row % 2 == 0, count[0], count[1]).astype(jnp.float32)
                 inverse = 1.0 / divisor
             both = jnp.concatenate(
-                [cache[i].reshape(4 * PAGE, HEAD) for i in (item, item + 1)], axis=1
+                [
+                    jnp.concatenate([cache[a, i].reshape(2 * PAGE, HEAD) for a in range(2)], axis=0)
+                    for i in (item, item + 1)
+                ],
+                axis=1,
             )
             total = jnp.dot(live, both, preferred_element_type=jnp.float32)
             for k in range(2):
                 mean = total[:, k * HEAD : (k + 1) * HEAD] * inverse
                 message[CTX.index(item + k), 2 * PAGE : ROWS, :] = mean[:TAIL].astype(jnp.bfloat16)
-            for i in (item, item + 1):
-                send(i).start(priority=i % 2)
-    for item in range(items):
-        send(item).wait()
+            ready.update((CTX.index(item), CTX.index(item + 1)))
+            for k, (at, size) in enumerate(SENDS):
+                if ready.issuperset(range(at, at + size)):
+                    send(k).start(priority=k % 2)
+                    ready.difference_update(range(at, at + size))
+    for k in range(len(SENDS)):
+        send(k).wait()
 
 
 def pack(page, counts, listed, cache_keys, cache_values):
     items = cache_keys.shape[0]
-    groups = items // 4
     whole = pl.BlockSpec(memory_space=pl.ANY)
     return pl.pallas_call(
         pack_kernel,
@@ -109,12 +119,12 @@
         out_specs=whole,
         out_shape=jax.ShapeDtypeStruct((items, ROWS, HEAD), jnp.bfloat16),
         scratch_shapes=[
-            pltpu.VMEM((items, 2, 2, PAGE, HEAD), jnp.bfloat16),
+            pltpu.VMEM((2, items, 2, PAGE, HEAD), jnp.bfloat16),
             pltpu.VMEM((items, ROWS, HEAD), jnp.bfloat16),
             pltpu.SMEM((counts.shape[0], HEAD), jnp.int32),
             pltpu.VMEM(listed.shape, jnp.int32),
-            pltpu.SemaphoreType.DMA((2, groups)),
-            pltpu.SemaphoreType.DMA((items,)),
+            pltpu.SemaphoreType.DMA((2, len(GROUPS))),
+            pltpu.SemaphoreType.DMA((len(SENDS),)),
             pltpu.SemaphoreType.DMA((2,)),
         ],
         compiler_params=pltpu.CompilerParams(vmem_limit_bytes=58 * MiB),
@@ -137,7 +147,7 @@
     out_ref,
     keys,
     values,
-    kb,
+    kt,
     vv,
     ckt,
     cv,
@@ -191,7 +201,7 @@
         for k in range(0, chunk, HEAD):
             start = pl.multiple_of(j * chunk + k, HEAD)
             at = pl.ds(start, HEAD)
-            kb[at, :] = keys[at, :].astype(jnp.bfloat16)
+            kt[:, at] = jnp.transpose(keys[at, :]).astype(jnp.bfloat16)
             vv[at, :HEAD] = values[at, :].astype(jnp.bfloat16)
             vv[at, HEAD:] = jnp.where(number + start < end, 1.0, 0.0).astype(jnp.bfloat16)
         return carry
@@ -215,11 +225,8 @@
         best[...] = score
 
         def scores(at, first=first):
-            score = lax.dot_general(
-                q_ref[first : first + block, :],
-                kb[at, :],
-                (((1,), (1,)), ((), ())),
-                preferred_element_type=jnp.float32,
+            score = jnp.dot(
+                q_ref[first : first + block, :], kt[:, at], preferred_element_type=jnp.float32
             )
             sc[:, at] = score
             parts = [score[:, k : k + HEAD] for k in range(0, at.size, HEAD)]
@@ -265,7 +272,7 @@
         scratch_shapes=[
             pltpu.VMEM((slots + chunk, HEAD), jnp.float32),
             pltpu.VMEM((slots + chunk, HEAD), jnp.float32),
-            pltpu.VMEM((slots, HEAD), jnp.bfloat16),
+            pltpu.VMEM((HEAD, slots), jnp.bfloat16),
             pltpu.VMEM((slots, 2 * HEAD), jnp.bfloat16),
             pltpu.VMEM((HEAD, cents), jnp.bfloat16),
             pltpu.VMEM((cents, 2 * HEAD), jnp.bfloat16),

time: 128 us -> 127 us (level)
  the two profiles are of different devices: /device:TPU:1 before, /device:TPU:12 now
where the time goes in v9:
time: 127 us
  waiting for transfers between devices  49.9 us (39%)
  blocking collectives  49.7 us (39%)
  Pallas kernels  12.5 us (10%)
  starting transfers between devices  10.7 us (8%)
  local copies, waits for them, and re-layouts  2.78 us (2%)
  other arithmetic  1.28 us (1%)
    all_to_all x1, waiting for transfers between devices, exchange(): lax.all_to_all(blocks, axis, split_axis=0, concat_axis=0, axis_index_grou...  49.9 us
    all_to_all x2, blocking collectives, exchange(): lax.all_to_all(blocks, axis, split_axis=0, concat_axis=0, axis_index_grou...  49.7 us
    all_to_all x1, starting transfers between devices, exchange(): lax.all_to_all(blocks, axis, split_axis=0, concat_axis=0, axis_index_grou...  10.7 us
    pallas_call x1, Pallas kernels, attend(): pl.pallas_call(functools.partial(attend_kernel, chunk=chunk, c=c), in_spe...  7.9 us
    pallas_call x1, Pallas kernels, pack(): pl.pallas_call(pack_kernel, in_specs=[pl.BlockSpec(memory_space=pltpu.SME...  4.05 us
  transfers between devices with their start and end apart: 1, of which 1 were waited for; matrix products, arithmetic and copies ran while one was open for 2% of the time, Pallas kernels for 0%

profile of v9, /device:TPU:12, one launch (start us, length us, event | category | flops | bytes accessed | tf_op | source)
XLA Modules:
  0.0 127.0 jit_solution(4184280864820248878)
XLA Ops:
  0.0 4.1 %pack.1 = bf16[64,136,128]{2,1,0:T(8,128)(2,1)} custom-call(s32[1]{0:T(128)} %bitcast.3.page_ref, s32[16,1024]{1,0:T(8,128)} %counts_ref.1, s32[64,256]{1,0:T(8,128)} %listed_ref.1, bf16[64,2,64,128]{3,2,1,0:T(8,128)(2,1)} %keys_ref.1, bf16[64,2,64,128]{3,2,1,0:T(8,128)(2,1)} %values_ref.1), custom_call_target="tpu_custom_call" | custom-call | tf_op jit(solution)/shard_map/pack/pallas_call | solution.py:116
  4.1 0.0 copy-start.1
  4.1 0.0 copy-start
  4.1 10.7 %all-to-all-start = ((bf16[64,136,128]{2,1,0:T(8,128)(2,1)}), bf16[64,136,128]{2,1,0:T(8,128)(2,1)S(1)}, u32[]{:S(2)}, u32[]{:S(2)}) async-start(bf16[64,136,128]{2,1,0:T(8,128)(2,1)} %pack.1), calls=%async_computation | async-start | bytes 4456448 | tf_op jit(solution)/shard_map/all_to_all | solution.py:330
  14.8 0.7 constant_dynamic-slice_fusion.1
  15.5 0.0 copy-done.1
  15.5 0.2 compare_reduce_fusion
  15.7 0.1 copy.33
  15.8 0.2 reduce_or.12
  16.0 0.8 dynamic-slice_reduce_fusion
  16.7 0.2 reshape.95
  17.0 0.1 copy.31
  17.1 0.1 fusion.8
  17.2 0.1 stack.5
  17.3 0.1 stack.6
  17.5 0.1 copy.34
  17.6 0.1 mul.42
  17.8 49.9 %all-to-all-done.got_ref = bf16[64,136,128]{2,1,0:T(8,128)(2,1)S(1)} async-done(((bf16[64,136,128]{2,1,0:T(8,128)(2,1)}), bf16[64,136,128]{2,1,0:T(8,128)(2,1)S(1)}, u32[]{:S(2)}, u32[]{:S(2)}) %all-to-all-start) | async-done | bytes 2228256 | tf_op jit(solution)/shard_map/all_to_all | solution.py:330
  67.6 0.0 copy-done
  67.6 7.9 %attend.1 = bf16[8,264,128]{2,1,0:T(8,128)(2,1)S(1)} custom-call(s32[64]{0:T(128)S(1)} %select_reduce_fusion.live_ref, f32[1,128]{1,0:T(1,128)S(1)} %broadcast_select_fusion.cbias_ref, bf16[64,136,128]{2,1,0:T(8,128)(2,1)S(1)} %all-to-all-done.got_ref, bf16[2048,128]{1,0:T(8,128)(2,1)S(1)} %bitcast.43), custom_call_target="tpu_custom_call" | custom-call | flops 4429185024 | bytes 4194304 | tf_op jit(solution)/shard_map/attend/pallas_call | solution.py:268
  75.5 28.7 %all_to_all.15.got_ref = bf16[8,264,128]{2,1,0:T(8,128)(2,1)S(1)} all-to-all(bf16[8,264,128]{2,1,0:T(8,128)(2,1)S(1)} %attend.1), channel_id=1, replica_groups={{0,3,6,1,4,7,2,5},{8,11,14,9,12,15,10,13},{16,19,22,17,20,23,18,21},{24..., dimensions={0} | all-to-all | bytes 1081344 | tf_op jit(solution)/shard_map/all_to_all | solution.py:330
  104.2 0.5 merge.1
  104.7 21.0 %all_to_all.16 = bf16[8,256,128]{2,1,0:T(8,128)(2,1)S(1)} all-to-all(bf16[8,256,128]{2,1,0:T(8,128)(2,1)S(1)} %merge.1), channel_id=1, replica_groups={{0,3,6,1,4,7,2,5},{8,11,14,9,12,15,10,13},{16,19,22,17,20,23,18,21},{24..., dimensions={0} | all-to-all | bytes 1048576 | tf_op jit(solution)/shard_map/all_to_all | solution.py:330
  125.9 1.0 convert.1
  (15 shorter events, 0.2 us)
Async XLA Ops:
  4.1 11.4 %copy-start.1 = (s32[64]{0:T(128)S(1)}, s32[64]{0:T(128)}, u32[]{:S(2)}) copy-start(s32[64]{0:T(128)} %constant.57) | copy-start | bytes 772
  4.1 63.5 %copy-start = (bf16[1,128,16,128]{3,2,1,0:T(8,128)(2,1)S(1)}, bf16[1,128,16,128]{3,2,1,0:T(8,128)(2,1)}, u32[]{:S(2)}) copy-start(bf16[1,128,16,128]{3,2,1,0:T(8,128)(2,1)} %param.10) | copy-start | bytes 1572868
  4.1 63.5 %all-to-all-start = ((bf16[64,136,128]{2,1,0:T(8,128)(2,1)}), bf16[64,136,128]{2,1,0:T(8,128)(2,1)S(1)}, u32[]{:S(2)}, u32[]{:S(2)}) async-start(bf16[64,136,128]{2,1,0:T(8,128)(2,1)} %pack.1), calls=%async_computation | async-start | bytes 4456448 | tf_op jit(solution)/shard_map/all_to_all | solution.py:330

commit v10 on v9

--- a/solution.py
+++ b/solution.py
@@ -191,7 +191,8 @@
     end = lax.fori_loop(0, sources, place, 0, unroll=4)
     half = chunk // 2
     halves = (end + half - 1) // half
-    chunks = halves // 2
+    large = 2 * chunk
+    whole_chunks = halves // 4
     rest = pl.ds(end, chunk)
     keys[rest, :] = jnp.broadcast_to(keys[0:1, :], (chunk, HEAD))
     values[rest, :] = jnp.zeros((chunk, HEAD), jnp.float32)
@@ -210,14 +211,20 @@
 
     def each_chunk(body):
         def whole(j, carry):
-            body(pl.ds(pl.multiple_of(j * chunk, chunk), chunk))
+            body(pl.ds(pl.multiple_of(j * large, large), large))
             return carry
 
-        lax.fori_loop(0, chunks, whole, 0)
-
-        @pl.when(halves % 2 == 1)
+        lax.fori_loop(0, whole_chunks, whole, 0)
+        left = halves % 4
+        done = whole_chunks * large
+
+        @pl.when(left >= 2)
         def _():
-            body(pl.ds(pl.multiple_of(chunks * chunk, chunk), half))
+            body(pl.ds(pl.multiple_of(done, chunk), chunk))
+
+        @pl.when(left % 2 == 1)
+        def _():
+            body(pl.ds(pl.multiple_of(done + (left // 2) * chunk, half), half))
 
     for first in range(0, q_ref.shape[0], block):
         score = jnp.dot(q_ref[first : first + block, :], ckt[...], preferred_element_type=jnp.float32) + cbias_ref[...]

time: 127 us -> 128 us (level); the launches traced: 127 us -> 126 us
  Pallas kernels: 12.5 us -> 10.4 us
  blocking collectives: 49.7 us -> 51.3 us
    pallas_call x1, Pallas kernels: 7.9 us -> 5.81 us  [attend(): pl.pallas_call(functools.partial(attend_kernel, chunk=chunk, c=c), in_spe...]
    all_to_all x2, blocking collectives: 49.7 us -> 51.3 us  [exchange(): lax.all_to_all(blocks, axis, split_axis=0, concat_axis=0, axis_index_grou...]
where the time goes in v10:
time: 128 us; the launch traced here: 126 us
  blocking collectives  51.3 us (40%)
  waiting for transfers between devices  49.9 us (39%)
  starting transfers between devices  10.7 us (8%)
  Pallas kernels  10.4 us (8%)
  local copies, waits for them, and re-layouts  2.78 us (2%)
  other arithmetic  1.28 us (1%)
    all_to_all x2, blocking collectives, exchange(): lax.all_to_all(blocks, axis, split_axis=0, concat_axis=0, axis_index_grou...  51.3 us
    all_to_all x1, waiting for transfers between devices, exchange(): lax.all_to_all(blocks, axis, split_axis=0, concat_axis=0, axis_index_grou...  49.9 us
    all_to_all x1, starting transfers between devices, exchange(): lax.all_to_all(blocks, axis, split_axis=0, concat_axis=0, axis_index_grou...  10.7 us
    pallas_call x1, Pallas kernels, attend(): pl.pallas_call(functools.partial(attend_kernel, chunk=chunk, c=c), in_spe...  5.81 us
    pallas_call x1, Pallas kernels, pack(): pl.pallas_call(pack_kernel, in_specs=[pl.BlockSpec(memory_space=pltpu.SME...  4.05 us
  transfers between devices with their start and end apart: 1, of which 1 were waited for; matrix products, arithmetic and copies ran while one was open for 2% of the time, Pallas kernels for 0%

profile of v10, /device:TPU:12, one launch (start us, length us, event | category | flops | bytes accessed | tf_op | source)
XLA Modules:
  0.0 126.4 jit_solution(17919453231323423839)
XLA Ops:
  0.0 4.1 %pack.1 = bf16[64,136,128]{2,1,0:T(8,128)(2,1)} custom-call(s32[1]{0:T(128)} %bitcast.3.page_ref, s32[16,1024]{1,0:T(8,128)} %counts_ref.1, s32[64,256]{1,0:T(8,128)} %listed_ref.1, bf16[64,2,64,128]{3,2,1,0:T(8,128)(2,1)} %keys_ref.1, bf16[64,2,64,128]{3,2,1,0:T(8,128)(2,1)} %values_ref.1), custom_call_target="tpu_custom_call" | custom-call | tf_op jit(solution)/shard_map/pack/pallas_call | solution.py:116
  4.1 0.0 copy-start.1
  4.1 0.0 copy-start
  4.1 10.7 %all-to-all-start = ((bf16[64,136,128]{2,1,0:T(8,128)(2,1)}), bf16[64,136,128]{2,1,0:T(8,128)(2,1)S(1)}, u32[]{:S(2)}, u32[]{:S(2)}) async-start(bf16[64,136,128]{2,1,0:T(8,128)(2,1)} %pack.1), calls=%async_computation | async-start | bytes 4456448 | tf_op jit(solution)/shard_map/all_to_all | solution.py:337
  14.8 0.7 constant_dynamic-slice_fusion.1
  15.5 0.0 copy-done.1
  15.5 0.2 compare_reduce_fusion
  15.7 0.1 copy.33
  15.8 0.2 reduce_or.12
  16.0 0.8 dynamic-slice_reduce_fusion
  16.7 0.2 reshape.95
  17.0 0.1 copy.31
  17.1 0.1 fusion.8
  17.2 0.1 stack.5
  17.3 0.1 stack.6
  17.5 0.1 copy.34
  17.6 0.1 mul.42
  17.8 49.9 %all-to-all-done.got_ref = bf16[64,136,128]{2,1,0:T(8,128)(2,1)S(1)} async-done(((bf16[64,136,128]{2,1,0:T(8,128)(2,1)}), bf16[64,136,128]{2,1,0:T(8,128)(2,1)S(1)}, u32[]{:S(2)}, u32[]{:S(2)}) %all-to-all-start) | async-done | bytes 2228256 | tf_op jit(solution)/shard_map/all_to_all | solution.py:337
  67.6 0.0 copy-done
  67.6 5.8 %attend.1 = bf16[8,264,128]{2,1,0:T(8,128)(2,1)S(1)} custom-call(s32[64]{0:T(128)S(1)} %select_reduce_fusion.live_ref, f32[1,128]{1,0:T(1,128)S(1)} %broadcast_select_fusion.cbias_ref, bf16[64,136,128]{2,1,0:T(8,128)(2,1)S(1)} %all-to-all-done.got_ref, bf16[2048,128]{1,0:T(8,128)(2,1)S(1)} %bitcast.43), custom_call_target="tpu_custom_call" | custom-call | flops 4429185024 | bytes 4194304 | tf_op jit(solution)/shard_map/attend/pallas_call | solution.py:275
  73.4 32.8 %all_to_all.15.got_ref = bf16[8,264,128]{2,1,0:T(8,128)(2,1)S(1)} all-to-all(bf16[8,264,128]{2,1,0:T(8,128)(2,1)S(1)} %attend.1), channel_id=1, replica_groups={{0,3,6,1,4,7,2,5},{8,11,14,9,12,15,10,13},{16,19,22,17,20,23,18,21},{24..., dimensions={0} | all-to-all | bytes 1081344 | tf_op jit(solution)/shard_map/all_to_all | solution.py:337
  106.3 0.5 merge.1
  106.8 18.4 %all_to_all.16 = bf16[8,256,128]{2,1,0:T(8,128)(2,1)S(1)} all-to-all(bf16[8,256,128]{2,1,0:T(8,128)(2,1)S(1)} %merge.1), channel_id=1, replica_groups={{0,3,6,1,4,7,2,5},{8,11,14,9,12,15,10,13},{16,19,22,17,20,23,18,21},{24..., dimensions={0} | all-to-all | bytes 1048576 | tf_op jit(solution)/shard_map/all_to_all | solution.py:337
  125.4 1.0 convert.1
  (15 shorter events, 0.2 us)
Async XLA Ops:
  4.1 11.4 %copy-start.1 = (s32[64]{0:T(128)S(1)}, s32[64]{0:T(128)}, u32[]{:S(2)}) copy-start(s32[64]{0:T(128)} %constant.57) | copy-start | bytes 772
  4.1 63.5 %copy-start = (bf16[1,128,16,128]{3,2,1,0:T(8,128)(2,1)S(1)}, bf16[1,128,16,128]{3,2,1,0:T(8,128)(2,1)}, u32[]{:S(2)}) copy-start(bf16[1,128,16,128]{3,2,1,0:T(8,128)(2,1)} %param.10) | copy-start | bytes 1572868
  4.1 63.5 %all-to-all-start = ((bf16[64,136,128]{2,1,0:T(8,128)(2,1)}), bf16[64,136,128]{2,1,0:T(8,128)(2,1)S(1)}, u32[]{:S(2)}, u32[]{:S(2)}) async-start(bf16[64,136,128]{2,1,0:T(8,128)(2,1)} %pack.1), calls=%async_computation | async-start | bytes 4456448 | tf_op jit(solution)/shard_map/all_to_all | solution.py:337
